TPU v7x, 128 devices: a whole 4x4x4 slice. The times are simulated.
128 devices in a mesh: row: 8 (over y_hi, z), col: 16 (over y_lo, x, core).
Axes of the slice: x: 4, y: 4 (y_hi: 2, y_lo: 2; y = y_hi * 2 + y_lo), z: 4, core: 2. Of those that a mesh axis runs over, the one named last changes fastest.
Arguments:
- transmission: float32 [2, 2, 2048, 8192], P(None, None, 'row', 'col'), may hold values from -1 to 1, as said below
- probe: float32 [2, 256, 256], replicated, may hold values from -6 to 6
- offsets: int32 [1024, 2], P(('row', 'col')), may hold values from 0 to 7936, as said below
- frames: int32 [1024, 256, 256], P(('row', 'col')), may hold values from 0 to 255
- lower_level: int32 [1024, 16, 16], P(('row', 'col')), may hold values from 0 to 7
- level_span: int32 [1024, 16, 16], P(('row', 'col')), may hold values from 0 to 15
Outputs:
- new_transmission: float32 [2, 2, 2048, 8192], P(None, None, 'row', 'col')
- new_probe: float32 [2, 256, 256], replicated
Inputs may be any that keep to these rules, and one draw needn't show every extreme that they name: `transmission`: real and imaginary parts of complex transmissions of modulus below 1. `offsets`: A position's patch anchor lies in the tile of rows 256 and columns 512 of the device that holds the position, and the whole 256 x 256 patch lies inside the region.
All inputs are finite; a program needn't handle non-finite values.
Results may differ from a plain program's by a relative error of at most 0.0003.
Values sent between devices are 32-bit elements; how exact they have to be, the bound alone decides.
A program may use at most 192 MiB of HBM per device.

v0:
```python
from functools import partial
import math

import jax
import jax.numpy as jnp
from jax import lax
from jax.sharding import PartitionSpec as P

PROPAGATION = 0.5
OBJECT_RATE = 0.1
PROBE_RATE = 0.5
HIGHEST = lax.Precision.HIGHEST


def from_behind(x, axis, by):
    length = lax.axis_size(axis)
    pairs = [(i, i + by) for i in range(length) if 0 <= i + by < length]
    return lax.ppermute(x, axis, pairs)


def kernel_parts(size):
    freq = jnp.arange(size, dtype=jnp.int32)
    freq = jnp.where(freq < size // 2, freq, freq - size)
    square = freq * freq
    total = square[:, None] + square[None, :]
    phase = total.astype(jnp.float32) * (-PROPAGATION * math.pi / size)
    return (jnp.cos(phase), jnp.sin(phase))


def dft_parts(size):
    index = jnp.arange(size, dtype=jnp.int32)
    product = index[:, None] * index[None, :] % size
    angle = product.astype(jnp.float32) * (2.0 * math.pi / size)
    factor = 1.0 / math.sqrt(size)
    return (jnp.cos(angle) * factor, jnp.sin(angle) * factor)


def intensity(counts, lower, span):
    blocks = lower.shape[-1]
    block = counts.shape[-1] // blocks
    base = 0.02 * jnp.exp2(lower.astype(jnp.float32) * 0.25)
    extent = 0.1 * jnp.exp2(span.astype(jnp.float32) * 0.25)
    shaped = counts.astype(jnp.float32).reshape(counts.shape[:-2] + (blocks, block, blocks, block))
    value = base[..., :, None, :, None] + shaped * (extent[..., :, None, :, None] / 255.0)
    return value.reshape(counts.shape)


def complex_mul(first, second):
    return (
        first[0] * second[0] - first[1] * second[1],
        first[0] * second[1] + first[1] * second[0],
    )


def conj_mul(first, second):
    return (
        first[0] * second[0] + first[1] * second[1],
        first[1] * second[0] - first[0] * second[1],
    )


def transform(values, cosine, sine, sign):
    left = partial(jnp.einsum, "pq,bqr->bpr", precision=HIGHEST)
    right = partial(jnp.einsum, "bpq,qr->bpr", precision=HIGHEST)
    table_imag = sine * sign
    real_mid = left(cosine, values[0]) - left(table_imag, values[1])
    imag_mid = left(cosine, values[1]) + left(table_imag, values[0])
    real_out = right(real_mid, cosine) - right(imag_mid, table_imag)
    imag_out = right(real_mid, table_imag) + right(imag_mid, cosine)
    return (real_out, imag_out)


def body(transmission, probe, offsets, frames, lower_level, level_span):
    layers = transmission.shape[0]
    tile_rows = transmission.shape[2]
    tile_cols = transmission.shape[3]
    width = probe.shape[-1]
    batch = offsets.shape[0]
    below = from_behind(transmission, "row", -1)
    taller = jnp.concatenate([transmission, below], 2)
    right = from_behind(taller[:, :, :, :width], "col", -1)
    extended = jnp.concatenate([taller, right], 3)
    anchor = jnp.stack([lax.axis_index("row") * tile_rows, lax.axis_index("col") * tile_cols])
    local = offsets - anchor[None, :]

    def take_patch(place):
        start = (jnp.int32(0), jnp.int32(0), place[0], place[1])
        return lax.dynamic_slice(extended, start, (layers, 2, width, width))

    patches = jax.vmap(take_patch)(local)
    cosine, sine = dft_parts(width)
    kernel_cos, kernel_sin = kernel_parts(width)

    def propagate(values, sign):
        spectrum = transform(values, cosine, sine, -1.0)
        turned = complex_mul(spectrum, (kernel_cos, sign * kernel_sin))
        return transform(turned, cosine, sine, 1.0)

    current = (
        jnp.broadcast_to(probe[0], (batch, width, width)),
        jnp.broadcast_to(probe[1], (batch, width, width)),
    )
    incoming = []
    for layer in range(layers):
        incoming.append(current)
        current = complex_mul(current, (patches[:, layer, 0], patches[:, layer, 1]))
        if layer < layers - 1:
            current = propagate(current, 1.0)
    far = transform(current, cosine, sine, -1.0)
    measured = intensity(frames, lower_level, level_span)
    misfit = far[0] * far[0] + far[1] * far[1] - measured
    back = transform((misfit * far[0], misfit * far[1]), cosine, sine, 1.0)
    pieces = [None] * layers
    for layer in reversed(range(layers)):
        pieces[layer] = jnp.stack(conj_mul(back, incoming[layer]), 1)
        back = conj_mul(back, (patches[:, layer, 0], patches[:, layer, 1]))
        if layer > 0:
            back = propagate(back, -1.0)
    gradient_patches = jnp.stack(pieces, 1)

    def accumulate(position, total):
        start = (jnp.int32(0), jnp.int32(0), local[position, 0], local[position, 1])
        current_patch = lax.dynamic_slice(total, start, (layers, 2, width, width))
        return lax.dynamic_update_slice(total, current_patch + gradient_patches[position], start)

    grad_extended = lax.fori_loop(0, batch, accumulate, jnp.zeros(extended.shape, jnp.float32))
    probe_local = jnp.stack([jnp.sum(back[0], 0), jnp.sum(back[1], 0)])
    probe_sum = lax.psum(probe_local, ("row", "col"))
    side = from_behind(grad_extended[:, :, :, tile_cols:], "col", 1)
    narrow = grad_extended[:, :, :, :tile_cols].at[:, :, :, :width].add(side)
    lower = from_behind(narrow[:, :, tile_rows:, :], "row", 1)
    gradient = narrow[:, :, :tile_rows, :].at[:, :, :width, :].add(lower)
    count_all = batch * lax.axis_size("row") * lax.axis_size("col")
    new_transmission = transmission - OBJECT_RATE * gradient
    new_probe = probe - PROBE_RATE / math.sqrt(count_all) * probe_sum
    return (new_transmission, new_probe.astype(jnp.float32))


def solution(mesh):
    in_specs = (
        P(None, None, "row", "col"),
        P(),
        P(("row", "col"), None),
        P(("row", "col"), None, None),
        P(("row", "col"), None, None),
        P(("row", "col"), None, None),
    )
    out_specs = (P(None, None, "row", "col"), P())
    return jax.shard_map(body, mesh=mesh, in_specs=in_specs, out_specs=out_specs, check_vma=False)
```

profile of v0, /device:TPU:1, one launch (start us, length us, event | category | flops | bytes accessed | tf_op | source)
XLA Modules:
  0.0 749.8 jit_solution(14635920521418714616)
XLA Ops:
  10.3 46.8 %collective-permute-done = f32[2,2,256,512]{3,2,1,0:T(8,128)S(1)} collective-permute-done((f32[2,2,256,512]{3,2,1,0:T(8,128)}, f32[2,2,256,512]{3,2,1,0:T(8,128)S(1)}, u32[]{:S(2)}, u32[]{:S(2)}) %collective-permute-start) | collective-permute-done | bytes 2097184 | tf_op jit(solution)/shard_map/ppermute | solution.py:18
  64.0 6.9 add.357
  70.9 11.4 %add.358 = f32[8,256,256]{2,1,0:T(8,128)S(1)} reshape(f32[8,16,16,16,16]{4,3,2,1,0:T(8,128)} %add.357) | data formatting | bytes 4194304 | tf_op jit(solution)/shard_map/add | solution.py:44
  82.4 6.9 mul.781
  89.3 12.5 %mul.782 = f32[8,256,256]{2,1,0:T(8,128)} reshape(f32[8,16,16,16,16]{4,3,2,1,0:T(8,128)} %mul.781) | data formatting | bytes 4194304 | tf_op jit(solution)/shard_map/mul | solution.py:44
  103.1 6.1 pad_maximum_fusion.1
  109.2 36.9 %while.18 = (s32[]{:T(128)}, f32[2,2,512,768]{3,2,1,0:T(8,128)}, s32[8,4]{0,1:T(4,128)S(1)}, f32[8,2,2,256,256]{4,3,0,2,1:T(8,128)}, s32[]{:T(128)}) while((s32[]{:T(128)}, f32[2,2,512,768]{3,2,1,0:T(8,128)}, s32[8,4]{0,1:T(4,128)S(1)}, f32[8,2,2,256,256]{4,3,0,2,1:T(8,128)}, s32[]{:T(128)}) %tuple.76), condition=%wide.while_cond.2, body=%wide.while_body.2.sunk | while | flops 2 | bytes 2098301 | solution.py:88
  146.1 6.9 fusion.158
  153.0 6.7 fusion.161
  159.7 4.8 convolution_add_fusion.5
  164.6 4.5 fusion.46
  169.0 4.5 fusion.48
  173.5 5.0 convolution_subtract_fusion.5
  178.6 4.5 fusion.63
  183.1 4.5 fusion.60
  187.6 4.8 fusion.103
  192.3 4.6 fusion.102
  197.0 4.8 convolution_add_fusion.4
  201.8 4.5 fusion.40
  210.8 5.0 convolution_subtract_fusion.4
  215.9 4.6 fusion.66
  220.4 5.1 fusion.34
  225.5 4.7 fusion.148
  234.6 4.8 convolution_add_fusion.3
  239.4 4.5 fusion.28
  244.0 4.5 fusion.26
  248.5 4.9 convolution_subtract_fusion.3
  253.5 4.6 fusion.72
  258.1 5.1 add_subtract_fusion
  263.2 4.7 fusion.100
  267.9 4.5 fusion.96
  272.4 4.7 convolution_add_fusion.2
  277.1 4.5 fusion.20
  281.6 4.5 fusion.18
  286.1 4.9 convolution_subtract_fusion.2
  291.1 4.5 fusion.78
  295.6 5.5 fusion.36
  301.0 4.7 fusion.138
  305.8 4.5 fusion.141
  310.3 4.7 convolution_add_fusion.1
  315.0 4.5 fusion.10
  319.5 4.5 fusion.12
  324.0 5.0 convolution_subtract_fusion.1
  329.0 4.6 fusion.87
  333.6 4.6 fusion.84
  338.1 4.8 fusion.105
  342.9 4.5 fusion.104
  347.4 4.6 convolution_add_fusion
  352.0 4.7 fusion.4
  356.7 4.6 fusion.2
  361.3 4.9 convolution_subtract_fusion
  370.8 5.5 fusion.57
  383.8 151.0 %while.17 = (s32[]{:T(128)}, f32[2,2,512,768]{3,2,1,0:T(8,128)}, s32[8,2]{0,1:T(2,128)S(1)}, f32[8,2,2,256,256]{4,3,0,2,1:T(8,128)}, s32[]{:T(128)}, /*index=5*/s32[]{:T(128)}, s32[]{:T(128)}, s32[]{:T(128)}) while((s32[]{:T(128)}, f32[2,2,512,768]{3,2,1,0:T(8,128)}, s32[8,2]{0,1:T(2,128)S(1)}, f32[8,2,2,256,256]{4,3,0,2,1:T(8,128)}, ...), condition=%wide.region_1.2_spmd, body=%wide.region_0.1_spmd.sunk | while | flops 262152 | bytes 5243077 | solution.py:126
  390.6 11.5 %dynamic_update_slice.8 = f32[2,2,512,768]{3,2,1,0:T(8,128)} dynamic-update-slice(f32[2,2,512,768]{3,2,1,0:T(8,128)} %get-tuple-element.252, f32[2,2,256,256]{3,2,1,0:T(8,128)S(1)} %bitcast_add_fusion.2, s32[]{:T(128)} %constant.140.clone.1..sunk, s32[]{:T(128)} %constant.140.clone.1..sunk, s32[]{:T(128)S(6)} %select_n.334, s32[]{:T(128)S(6)} %select_n.335) | dynamic-update-slice | bytes 2097156 | tf_op jit(solution)/shard_map/while/body/eval_jaxpr/dynamic_update_slice | solution.py:124
  409.0 12.3 %dynamic_update_slice.8 = f32[2,2,512,768]{3,2,1,0:T(8,128)} dynamic-update-slice(f32[2,2,512,768]{3,2,1,0:T(8,128)} %get-tuple-element.252, f32[2,2,256,256]{3,2,1,0:T(8,128)S(1)} %bitcast_add_fusion.2, s32[]{:T(128)} %constant.140.clone.1..sunk, s32[]{:T(128)} %constant.140.clone.1..sunk, s32[]{:T(128)S(6)} %select_n.334, s32[]{:T(128)S(6)} %select_n.335) | dynamic-update-slice | bytes 2097156 | tf_op jit(solution)/shard_map/while/body/eval_jaxpr/dynamic_update_slice | solution.py:124
  428.1 12.2 %dynamic_update_slice.8 = f32[2,2,512,768]{3,2,1,0:T(8,128)} dynamic-update-slice(f32[2,2,512,768]{3,2,1,0:T(8,128)} %get-tuple-element.252, f32[2,2,256,256]{3,2,1,0:T(8,128)S(1)} %bitcast_add_fusion.2, s32[]{:T(128)} %constant.140.clone.1..sunk, s32[]{:T(128)} %constant.140.clone.1..sunk, s32[]{:T(128)S(6)} %select_n.334, s32[]{:T(128)S(6)} %select_n.335) | dynamic-update-slice | bytes 2097156 | tf_op jit(solution)/shard_map/while/body/eval_jaxpr/dynamic_update_slice | solution.py:124
  447.1 12.1 %dynamic_update_slice.8 = f32[2,2,512,768]{3,2,1,0:T(8,128)} dynamic-update-slice(f32[2,2,512,768]{3,2,1,0:T(8,128)} %get-tuple-element.252, f32[2,2,256,256]{3,2,1,0:T(8,128)S(1)} %bitcast_add_fusion.2, s32[]{:T(128)} %constant.140.clone.1..sunk, s32[]{:T(128)} %constant.140.clone.1..sunk, s32[]{:T(128)S(6)} %select_n.334, s32[]{:T(128)S(6)} %select_n.335) | dynamic-update-slice | bytes 2097156 | tf_op jit(solution)/shard_map/while/body/eval_jaxpr/dynamic_update_slice | solution.py:124
  466.0 12.2 %dynamic_update_slice.8 = f32[2,2,512,768]{3,2,1,0:T(8,128)} dynamic-update-slice(f32[2,2,512,768]{3,2,1,0:T(8,128)} %get-tuple-element.252, f32[2,2,256,256]{3,2,1,0:T(8,128)S(1)} %bitcast_add_fusion.2, s32[]{:T(128)} %constant.140.clone.1..sunk, s32[]{:T(128)} %constant.140.clone.1..sunk, s32[]{:T(128)S(6)} %select_n.334, s32[]{:T(128)S(6)} %select_n.335) | dynamic-update-slice | bytes 2097156 | tf_op jit(solution)/shard_map/while/body/eval_jaxpr/dynamic_update_slice | solution.py:124
  485.0 11.9 %dynamic_update_slice.8 = f32[2,2,512,768]{3,2,1,0:T(8,128)} dynamic-update-slice(f32[2,2,512,768]{3,2,1,0:T(8,128)} %get-tuple-element.252, f32[2,2,256,256]{3,2,1,0:T(8,128)S(1)} %bitcast_add_fusion.2, s32[]{:T(128)} %constant.140.clone.1..sunk, s32[]{:T(128)} %constant.140.clone.1..sunk, s32[]{:T(128)S(6)} %select_n.334, s32[]{:T(128)S(6)} %select_n.335) | dynamic-update-slice | bytes 2097156 | tf_op jit(solution)/shard_map/while/body/eval_jaxpr/dynamic_update_slice | solution.py:124
  503.7 12.0 %dynamic_update_slice.8 = f32[2,2,512,768]{3,2,1,0:T(8,128)} dynamic-update-slice(f32[2,2,512,768]{3,2,1,0:T(8,128)} %get-tuple-element.252, f32[2,2,256,256]{3,2,1,0:T(8,128)S(1)} %bitcast_add_fusion.2, s32[]{:T(128)} %constant.140.clone.1..sunk, s32[]{:T(128)} %constant.140.clone.1..sunk, s32[]{:T(128)S(6)} %select_n.334, s32[]{:T(128)S(6)} %select_n.335) | dynamic-update-slice | bytes 2097156 | tf_op jit(solution)/shard_map/while/body/eval_jaxpr/dynamic_update_slice | solution.py:124
  522.5 12.3 %dynamic_update_slice.8 = f32[2,2,512,768]{3,2,1,0:T(8,128)} dynamic-update-slice(f32[2,2,512,768]{3,2,1,0:T(8,128)} %get-tuple-element.252, f32[2,2,256,256]{3,2,1,0:T(8,128)S(1)} %bitcast_add_fusion.2, s32[]{:T(128)} %constant.140.clone.1..sunk, s32[]{:T(128)} %constant.140.clone.1..sunk, s32[]{:T(128)S(6)} %select_n.334, s32[]{:T(128)S(6)} %select_n.335) | dynamic-update-slice | bytes 2097156 | tf_op jit(solution)/shard_map/while/body/eval_jaxpr/dynamic_update_slice | solution.py:124
  541.1 20.3 %collective-permute-done.2 = f32[2,2,512,256]{3,2,1,0:T(8,128)S(1)} collective-permute-done((f32[2,2,512,256]{3,2,1,0:T(8,128)S(1)}, f32[2,2,512,256]{3,2,1,0:T(8,128)S(1)}, u32[]{:S(2)}, u32[]{:S(2)}) %collective-permute-start.2) | collective-permute-done | bytes 2097184 | tf_op jit(solution)/shard_map/ppermute | solution.py:18
  565.9 6.4 collective-permute-start.3
  573.1 163.4 %all-reduce.2.cloned.1.call-done = f32[2,256,256]{2,1,0:T(8,128)} async-done(((f32[2,256,256]{2,1,0:T(8,128)}), f32[2,256,256]{2,1,0:T(8,128)}) %all-reduce.2.cloned.1.call-update) | async-done | bytes 524304 | tf_op jit(solution)/shard_map/psum | solution.py:128
  (98 shorter events, 109.2 us)
Async XLA Ops:
  7.2 729.3 %all-reduce.2.cloned.1.call-start = ((), (), s32[]{:S(2)}) async-start(), calls=%async_computation | async-start | bytes 1048576 | tf_op jit(solution)/shard_map/psum | solution.py:128
  7.2 49.9 %collective-permute-start = (f32[2,2,256,512]{3,2,1,0:T(8,128)}, f32[2,2,256,512]{3,2,1,0:T(8,128)S(1)}, u32[]{:S(2)}, u32[]{:S(2)}) collective-permute-start(f32[2,2,256,512]{3,2,1,0:T(8,128)} %param.14), channel_id=1, source_target_pairs={{16,0},{32,16},{48,32},{64,48},{80,64},{96,80},{112,96},{17,1},{33... | collective-permute-start | bytes 6291464 | tf_op jit(solution)/shard_map/ppermute | solution.py:18
  57.3 2.0 copy-start.1
  59.3 4.7 copy-start.8
  60.8 42.3 %collective-permute-start.1 = (f32[2,2,512,256]{3,2,1,0:T(8,128)}, f32[2,2,512,256]{3,2,1,0:T(8,128)}, u32[]{:S(2)}, u32[]{:S(2)}) collective-permute-start(f32[2,2,512,256]{3,2,1,0:T(8,128)} %slice.130), channel_id=1, source_target_pairs={{1,0},{2,1},{3,2},{4,3},{5,4},{6,5},{7,6},{8,7},{9,8},{10,9},{11,1... | collective-permute-start | bytes 6291464 | tf_op jit(solution)/shard_map/ppermute | solution.py:18
  70.9 11.4 %copy-start.9 = (s32[8,16,16]{2,1,0:T(8,128)S(1)}, s32[8,16,16]{2,1,0:T(8,128)}, u32[]{:S(2)}) copy-start(s32[8,16,16]{2,1,0:T(8,128)} %param.19) | copy-start | bytes 24580
  89.3 12.6 %copy-start.10 = (s32[8,2]{0,1:T(2,128)S(1)}, s32[8,2]{0,1:T(2,128)}, u32[]{:S(2)}) copy-start(s32[8,2]{0,1:T(2,128)} %param.16) | copy-start | bytes 196
  89.3 12.8 %copy-start.5 = (f32[2,256,256]{2,1,0:T(8,128)S(1)}, f32[2,256,256]{2,1,0:T(8,128)}, u32[]{:S(2)}) copy-start(f32[2,256,256]{2,1,0:T(8,128)} %param.15) | copy-start | bytes 1572868
  146.1 13.7 %copy-start = (f32[8,2,2,256,256]{4,3,0,2,1:T(8,128)S(1)}, f32[8,2,2,256,256]{4,3,0,2,1:T(8,128)}, u32[]{:S(2)}) copy-start(f32[8,2,2,256,256]{4,3,0,2,1:T(8,128)} %get-tuple-element.121) | copy-start | bytes 25165828
  253.4 4.6 copy-start.4
  253.5 4.6 copy-start.7
  536.5 24.9 %collective-permute-start.2 = (f32[2,2,512,256]{3,2,1,0:T(8,128)S(1)}, f32[2,2,512,256]{3,2,1,0:T(8,128)S(1)}, u32[]{:S(2)}, u32[]{:S(2)}) collective-permute-start(f32[2,2,512,256]{3,2,1,0:T(8,128)S(1)} %slice.108), channel_id=1, source_target_pairs={{0,1},{1,2},{2,3},{3,4},{4,5},{5,6},{6,7},{7,8},{8,9},{9,10},{10,1... | collective-permute-start | bytes 6291464 | tf_op jit(solution)/shard_map/ppermute | solution.py:18
  563.3 2.6 copy-start.2
  563.3 173.2 %copy-start.6 = (f32[2,256,256]{2,1,0:T(8,128)S(1)}, f32[2,256,256]{2,1,0:T(8,128)}, u32[]{:S(2)}) copy-start(f32[2,256,256]{2,1,0:T(8,128)} %param.15) | copy-start | bytes 1572868
  565.9 172.5 %copy-start.3 = (f32[2,2,256,512]{3,2,1,0:T(8,128)S(1)}, f32[2,2,256,512]{3,2,1,0:T(8,128)}, u32[]{:S(2)}) copy-start(f32[2,2,256,512]{3,2,1,0:T(8,128)} %param.14) | copy-start | bytes 6291460
  565.9 172.5 %collective-permute-start.3 = (f32[2,2,256,512]{3,2,1,0:T(8,128)}, f32[2,2,256,512]{3,2,1,0:T(8,128)}, u32[]{:S(2)}, u32[]{:S(2)}) collective-permute-start(f32[2,2,256,512]{3,2,1,0:T(8,128)} %slice.132), channel_id=1, source_target_pairs={{0,16},{16,32},{32,48},{48,64},{64,80},{80,96},{96,112},{1,17},{17... | collective-permute-start | bytes 6291464 | tf_op jit(solution)/shard_map/ppermute | solution.py:18
Sparse Core Ops, SparseCore 0:
  573.2 163.2 all-reduce.1
where the time goes:
time: 760 us; the launch traced here: 750 us
  waiting for transfers between devices  231 us (30%)
  matrix products  229 us (30%)
  local copies, waits for them, and re-layouts  192 us (25%)
  other arithmetic  37.8 us (5%)
  loops' own time  32.3 us (4%)
  between operations  14.8 us (2%)
  starting transfers between devices  12.8 us (2%)
    psum x1, waiting for transfers between devices, body(): probe_sum = lax.psum(probe_local, ('row', 'col'))  163 us
    dynamic_update_slice x8, local copies, waits for them, and re-layouts, accumulate(): lax.dynamic_update_slice(total, current_patch + gradient_patches[position...  96.5 us
    ppermute x4, waiting for transfers between devices, from_behind(): return lax.ppermute(x, axis, pairs)  67.1 us
    dot_general x12, matrix products, transform(): real_mid = left(cosine, values[0]) - left(table_imag, values[1])  59.3 us
    dot_general x12, matrix products, transform(): imag_mid = left(cosine, values[1]) + left(table_imag, values[0])  58.8 us
    dot_general x12, matrix products, transform(): imag_out = right(real_mid, table_imag) + right(imag_mid, cosine)  57.1 us
    dot_general x12, matrix products, transform(): real_out = right(real_mid, cosine) - right(imag_mid, table_imag)  54.2 us
    gather x24, local copies, waits for them, and re-layouts  36.7 us
  transfers between devices with their start and end apart: 5, of which 3 were waited for; matrix products, arithmetic and copies ran while one was open for 6% of the time, Pallas kernels for 0%

commit v1 on v0

v1 whole, which is shorter than its diff:
```python
import functools
import math

import jax
import jax.numpy as jnp
import numpy as np
from jax import lax
from jax.experimental import pallas as pl
from jax.experimental.pallas import tpu as pltpu
from jax.sharding import PartitionSpec as P

PROPAGATION = 0.5
OBJECT_RATE = 0.1
PROBE_RATE = 0.5
N = 256
HALF = 128
NBK = 16
DIMS = dict(yh=2, z=4, yl=2, x=4, core=2)
MESH = pl.DeviceIdType.MESH
F32 = jnp.float32
BF16 = jnp.bfloat16


def block_pairs():
    n = np.arange(N)
    dft = np.exp(-2j * np.pi * np.outer(n, n) / N) / math.sqrt(N)
    freq = np.where(n < HALF, n, n - N).astype(np.float64)
    chirp = np.exp(-1j * np.pi * PROPAGATION * freq * freq / N)
    prop = dft.conj().T @ (chirp[:, None] * dft)
    fu, fv = dft[0::2, :HALF], dft[1::2, :HALF]
    first, second = prop[:HALF, :HALF], prop[:HALF, HALF:]
    cu, cv = (first + second) / 2, (first - second) / 2
    return {
        "prop": (cu, cv),
        "dft": (fu, fv),
        "idft": (fu.conj().T, fv.conj().T),
        "adj": (cu.conj().T, cv.conj().T),
    }


ORDER = ("prop", "dft", "idft", "adj")


def tables():
    left, right = [], []
    pairs = block_pairs()
    for name in ORDER:
        for m in pairs[name]:
            real = np.block([[m.real, -m.imag], [m.imag, m.real]]).astype(np.float32)
            hi = np.asarray(real, dtype=jnp.bfloat16)
            lo = np.asarray(real - hi.astype(np.float32), dtype=jnp.bfloat16)
            left.append(np.concatenate([hi, hi, lo], 1))
            right.append(np.concatenate([hi.T, hi.T, lo.T], 0))
    return np.stack(left), np.stack(right)


def permutation():
    perm = np.zeros((N, N), np.float32)
    for p in range(N):
        perm[p, 2 * p if p < HALF else 2 * (p - HALF) + 1] = 1
    rows = np.asarray(perm, dtype=jnp.bfloat16)
    cols = np.asarray(perm.T, dtype=jnp.bfloat16)
    spread = np.zeros((NBK, N), np.float32)
    for p in range(N):
        spread[(p % HALF) // 8, p] = 1
    return rows, cols, spread


def split(x):
    hi = x.astype(BF16)
    lo = (x - hi.astype(F32)).astype(BF16)
    return hi, lo


def dot(a, b):
    return jnp.dot(a, b, preferred_element_type=F32)


def along_cols(re, im, right_ref, op, pre, post):
    a, b, c, d = re[:, :HALF], re[:, HALF:], im[:, :HALF], im[:, HALF:]
    if pre:
        u = jnp.concatenate([a + b, c + d], 1)
        v = jnp.concatenate([a - b, c - d], 1)
    else:
        u = jnp.concatenate([a, c], 1)
        v = jnp.concatenate([b, d], 1)
    out = []
    for i, x in enumerate((u, v)):
        hi, lo = split(x)
        out.append(dot(jnp.concatenate([hi, lo, hi], 1), right_ref[2 * op + i]))
    yu, yv = out
    if post:
        p, m = yu + yv, yu - yv
    else:
        p, m = yu, yv
    return (
        jnp.concatenate([p[:, :HALF], m[:, :HALF]], 1),
        jnp.concatenate([p[:, HALF:], m[:, HALF:]], 1),
    )


def along_rows(re, im, left_ref, op, pre, post):
    a, b, c, d = re[:HALF], re[HALF:], im[:HALF], im[HALF:]
    if pre:
        u = jnp.concatenate([a + b, c + d], 0)
        v = jnp.concatenate([a - b, c - d], 0)
    else:
        u = jnp.concatenate([a, c], 0)
        v = jnp.concatenate([b, d], 0)
    out = []
    for i, x in enumerate((u, v)):
        hi, lo = split(x)
        out.append(dot(left_ref[2 * op + i], jnp.concatenate([hi, lo, hi], 0)))
    yu, yv = out
    if post:
        p, m = yu + yv, yu - yv
    else:
        p, m = yu, yv
    return (
        jnp.concatenate([p[:HALF], m[:HALF]], 0),
        jnp.concatenate([p[HALF:], m[HALF:]], 0),
    )


def transform(re, im, left_ref, right_ref, op, pre, post):
    re, im = along_cols(re, im, right_ref, op, pre, post)
    return along_rows(re, im, left_ref, op, pre, post)


def complex_mul(a, b):
    return a[0] * b[0] - a[1] * b[1], a[0] * b[1] + a[1] * b[0]


def conj_mul(a, b):
    return a[0] * b[0] + a[1] * b[1], a[1] * b[0] - a[0] * b[1]


def kernel(
    batch,
    rate,
    dims,
    place_ref,
    trans_hbm,
    probe_ref,
    frames_hbm,
    lower_ref,
    span_ref,
    left_hbm,
    right_hbm,
    perm_rows_ref,
    perm_cols_ref,
    spread_ref,
    grad_ref,
    newprobe_ref,
    own0,
    own1,
    bel0,
    bel1,
    gown0,
    gown1,
    gbel0,
    gbel1,
    rin0,
    rin1,
    din0,
    din1,
    frames,
    left,
    right,
    meas,
    wav,
    patch0,
    amp,
    piece,
    gacc,
    stage_core,
    stage_x,
    stage_y,
    stage_z,
    local_sem,
    send_sem,
    recv_sem,
):
    own, bel = (own0, own1), (bel0, bel1)
    gown, gbel = (gown0, gown1), (gbel0, gbel1)
    rin, din = (rin0, rin1), (din0, din1)
    n_z, n_x, n_yl, n_yh = dims["z"], dims["x"], dims["yl"], dims["yh"]
    n_row, n_col = n_yh * n_z, n_yl * n_x * 2
    row, col = lax.axis_index("row"), lax.axis_index("col")
    yh, z = row // n_z, row % n_z
    yl, x, core = col // (2 * n_x), (col // 2) % n_x, col % 2
    y_digit = yh * n_yl + yl
    n_y = n_yh * n_yl

    has_up, has_down = row > 0, row < n_row - 1
    has_left, has_right = col > 0, col < n_col - 1
    up, down = (row - 1, col), (row + 1, col)
    lft, rgt = (row, col - 1), (row, col + 1)

    def core_member(m):
        return (row, yl * 2 * n_x + x * 2 + m)

    def x_member(m):
        return (row, yl * 2 * n_x + m * 2 + core)

    def y_member(m):
        return ((m // n_yl) * n_z + z, (m % n_yl) * 2 * n_x + x * 2 + core)

    def z_member(m):
        return (yh * n_z + m, col)

    def load(src, dst, i):
        return pltpu.make_async_copy(src, dst, local_sem.at[i])

    loads = []
    for s in range(2):
        for c in range(2):
            loads.append(
                load(trans_hbm.at[s, :, :, pl.ds(c * N, N)], own[s].at[c], 2 * s + c)
            )
    loads.append(load(frames_hbm, frames, 4))
    loads.append(load(left_hbm, left, 5))
    loads.append(load(right_hbm, right, 6))
    for c in loads:
        c.start()

    barrier = pltpu.get_barrier_semaphore()

    def hail(dev):
        pl.semaphore_signal(barrier, inc=1, device_id=dev, device_id_type=MESH)

    for cond, dev in (
        (has_up, up),
        (has_down, down),
        (has_left, lft),
        (has_right, rgt),
    ):

        @pl.when(cond)
        def _(dev=dev):
            hail(dev)

    groups = (
        (core_member, 2, core),
        (x_member, n_x, x),
        (y_member, n_y, y_digit),
        (z_member, n_z, z),
    )
    for member, size, me in groups:
        for k in range(1, size):
            hail(member((me + k) % size))
    hails = sum(size - 1 for _, size, _ in groups)
    for cond in (has_up, has_down, has_left, has_right):
        hails = hails + jnp.where(cond, 1, 0)
    pl.semaphore_wait(barrier, hails)

    def remote(src, dst, i, dev):
        return pltpu.make_async_remote_copy(
            src_ref=src,
            dst_ref=dst,
            send_sem=send_sem.at[i],
            recv_sem=recv_sem.at[i],
            device_id=dev,
            device_id_type=MESH,
        )

    def fwd_rows(s, c):
        return remote(
            trans_hbm.at[s, :, :, pl.ds(c * N, N)], bel[s].at[c], 8 * s + c, up
        )

    def fwd_side(s):
        return remote(trans_hbm.at[s, :, :, pl.ds(0, N)], own[s].at[2], 8 * s + 2, lft)

    def fwd_corner(s):
        return remote(bel[s].at[0], bel[s].at[2], 8 * s + 3, lft)

    def back_corner(s):
        return remote(gbel[s].at[2], rin[s].at[1], 8 * s + 4, rgt)

    def back_side(s):
        return remote(gown[s].at[2], rin[s].at[0], 8 * s + 5, rgt)

    def back_rows(s, c):
        return remote(gbel[s].at[c], din[s].at[c], 8 * s + 6 + c, down)

    def on(cond, f):
        @pl.when(cond)
        def _():
            f()

    for c in range(2):
        on(has_up, fwd_rows(0, c).start)
    on(has_left, fwd_side(0).start)

    zero3 = jnp.zeros((2, N, N), F32)
    for s in range(2):

        @pl.when(jnp.logical_not(has_down))
        def _(s=s):
            for c in range(3):
                bel[s][c] = zero3

        @pl.when(jnp.logical_not(has_right))
        def _(s=s):
            own[s][2] = zero3
            on(has_down, functools.partial(bel[s].__setitem__, 2, zero3))

        @pl.when(jnp.logical_not(has_up))
        def _(s=s):
            for c in range(2):
                din[s][c] = zero3

        @pl.when(jnp.logical_not(has_left))
        def _(s=s):
            for c in range(2):
                rin[s][c] = zero3

    loads[4].wait()
    for c in loads[5:]:
        c.wait()

    def place(j):
        return place_ref[2 * j], place_ref[2 * j + 1]

    @pl.loop(0, batch)
    def _(j):
        counts = frames[j].astype(F32).astype(BF16)
        mixed = dot(perm_rows_ref[...], counts).astype(BF16)
        counts = dot(mixed, perm_cols_ref[...])
        base = 0.02 * jnp.exp2(lower_ref[j].astype(F32) * 0.25)
        extent = (0.1 / 255.0) * jnp.exp2(span_ref[j].astype(F32) * 0.25)

        def widen(small):
            wide = jnp.dot(
                small,
                spread_ref[...],
                precision=lax.Precision.HIGHEST,
                preferred_element_type=F32,
            )
            tall = jnp.broadcast_to(wide[:, None, :], (NBK, 8, N)).reshape(HALF, N)
            return jnp.concatenate([tall, tall], 0)

        meas[j] = widen(base) + counts * widen(extent)
        y, x = place(j)
        shift = x % N
        for p in range(2):
            wav[j, p] = pltpu.roll(pltpu.roll(probe_ref[p], shift, 1), y, 0)

    def masks(j):
        y, x = place(j)
        rows = lax.broadcasted_iota(jnp.int32, (N, N), 0) >= y
        cols = lax.broadcasted_iota(jnp.int32, (N, N), 1) >= x % N
        return rows, cols, x // N

    def take(s, j, p):
        rows, cols, k = masks(j)
        here = jnp.where(cols, own[s][k, p], own[s][k + 1, p])
        below = jnp.where(cols, bel[s][k, p], bel[s][k + 1, p])
        return jnp.where(rows, here, below)

    def arrive(s):
        @pl.when(has_down)
        def _():
            fwd_rows(s, 0).wait_recv()

        @pl.when(jnp.logical_and(has_down, has_left))
        def _():
            fwd_corner(s).start()

        if s == 0:
            for c in range(2):
                on(has_up, fwd_rows(1, c).start)
            on(has_left, fwd_side(1).start)

        @pl.when(has_down)
        def _():
            fwd_rows(s, 1).wait_recv()

        @pl.when(has_right)
        def _():
            fwd_side(s).wait_recv()

        @pl.when(jnp.logical_and(has_down, has_right))
        def _():
            fwd_corner(s).wait_recv()

    for c in loads[:4]:
        c.wait()
    arrive(0)

    @pl.loop(0, batch)
    def _(j):
        patch = take(0, j, 0), take(0, j, 1)
        patch0[j, 0], patch0[j, 1] = patch
        wave = complex_mul((wav[j, 0], wav[j, 1]), patch)
        amp[j, 0], amp[j, 1] = transform(*wave, left, right, 0, True, True)

    arrive(1)

    @pl.loop(0, batch)
    def _(j):
        patch = take(1, j, 0), take(1, j, 1)
        incoming = amp[j, 0], amp[j, 1]
        far = transform(*complex_mul(incoming, patch), left, right, 1, True, False)
        misfit = far[0] * far[0] + far[1] * far[1] - meas[j]
        back = transform(misfit * far[0], misfit * far[1], left, right, 2, False, True)
        piece[j, 0], piece[j, 1] = conj_mul(back, incoming)
        amp[j, 0], amp[j, 1] = conj_mul(back, patch)

    def accumulate(s):
        @pl.loop(0, N // 8)
        def _(i):
            here = pl.ds(pl.multiple_of(i * 8, 8), 8)
            rows = lax.broadcasted_iota(jnp.int32, (8, N), 0) + i * 8
            cols = lax.broadcasted_iota(jnp.int32, (8, N), 1)
            for p in range(2):
                sums = [[jnp.zeros((8, N), F32) for _ in range(3)] for _ in range(2)]
                for j in range(batch):
                    y, x = place(j)
                    value = piece[j, p, here, :]
                    target = x // N + jnp.where(cols >= x % N, 0, 1)
                    upper = jnp.where(rows >= y, value, 0.0)
                    for r, part in enumerate((upper, value - upper)):
                        for c in range(3):
                            sums[r][c] += jnp.where(target == c, part, 0.0)
                for c in range(3):
                    gown[s][c, p, here, :] = sums[0][c]
                    gbel[s][c, p, here, :] = sums[1][c]

    def send_back(s):
        on(has_right, back_corner(s).start)
        on(has_down, back_rows(s, 1).start)
        on(has_right, back_side(s).start)

    def send_back_late(s):
        @pl.when(has_left)
        def _():
            back_corner(s).wait_recv()

        gbel[s][0] += rin[s][1]
        on(has_down, back_rows(s, 0).start)

    accumulate(1)
    send_back(1)
    send_back_late(1)

    gacc[...] = jnp.zeros_like(gacc)

    @pl.loop(0, batch)
    def _(j):
        back = transform(amp[j, 0], amp[j, 1], left, right, 3, True, True)
        piece[j, 0], piece[j, 1] = conj_mul(back, (wav[j, 0], wav[j, 1]))
        term = conj_mul(back, (patch0[j, 0], patch0[j, 1]))
        y, x = place(j)
        for p in range(2):
            turned = pltpu.roll(pltpu.roll(term[p], (N - y) % N, 0), (N - x % N) % N, 1)
            for h in range(2):
                gacc[pl.ds((2 * p + h) * N, N), :] += turned[:, h * HALF : (h + 1) * HALF]

    accumulate(0)
    send_back(0)
    send_back_late(0)

    total = gacc.shape[0]
    stages = (
        (stage_core, core_member, 2, core, 16),
        (stage_x, x_member, n_x, x, 18),
        (stage_y, y_member, n_y, y_digit, 22),
        (stage_z, z_member, n_z, z, 26),
    )
    length = total
    base = 0
    spans = []
    for stage, member, size, me, sem in stages:
        chunk = length // size
        copies = []
        for k in range(1, size):
            m = (me + k) % size
            src = gacc.at[pl.ds(pl.multiple_of(base + m * chunk, 8), chunk), :]
            copies.append(remote(src, stage.at[k - 1], sem + k - 1, member(m)))
        for c in copies:
            c.start()
        spans.append((base, length, chunk))
        base = base + me * chunk
        mine = pl.ds(pl.multiple_of(base, 8), chunk)
        for c in copies:
            c.wait()
        got = gacc[mine, :]
        for k in range(1, size):
            got = got + stage[k - 1]
        gacc[mine, :] = got
        length = chunk

    mine = pl.ds(pl.multiple_of(base, 8), length)
    newprobe_ref[mine, :] = gacc[mine, :]
    for (stage, member, size, me, sem), (start, length, chunk) in reversed(
        list(zip(stages, spans))
    ):
        held = newprobe_ref.at[pl.ds(pl.multiple_of(start + me * chunk, 8), chunk), :]
        copies = [
            remote(held, held, 14 + sem + k - 1, member((me + k) % size))
            for k in range(1, size)
        ]
        for c in copies:
            c.start()
        for k, c in enumerate(copies, 1):
            c.wait_send()
            m = (me - k + size) % size
            there = newprobe_ref.at[pl.ds(pl.multiple_of(start + m * chunk, 8), chunk), :]
            remote(there, there, 14 + sem + k - 1, member(m)).wait_recv()

    for s in (1, 0):

        @pl.when(has_left)
        def _(s=s):
            back_side(s).wait_recv()

        for c in range(2):

            @pl.when(has_up)
            def _(s=s, c=c):
                back_rows(s, c).wait_recv()

            for p in range(2):
                value = gown[s][c, p] + din[s][c, p]
                if c == 0:
                    value = value + rin[s][0, p]
                grad_ref[s, p, :, pl.ds(c * N, N)] = value

    for s in range(2):
        for c in range(2):
            on(has_up, fwd_rows(s, c).wait_send)
            on(has_down, back_rows(s, c).wait_send)
        on(has_left, fwd_side(s).wait_send)
        on(jnp.logical_and(has_down, has_left), fwd_corner(s).wait_send)
        on(has_right, back_corner(s).wait_send)
        on(has_right, back_side(s).wait_send)


def body(dims, transmission, probe, offsets, frames, lower_level, level_span):
    batch = offsets.shape[0]
    layers, _, rows, cols = transmission.shape
    anchor = jnp.stack([lax.axis_index("row") * rows, lax.axis_index("col") * cols])
    place = (offsets - anchor[None, :]).reshape(2 * batch)
    left, right = tables()
    perm_rows, perm_cols, spread = permutation()
    n_y = dims["yh"] * dims["yl"]
    total = 2 * 2 * N
    chunk_core = total // 2
    chunk_x = chunk_core // dims["x"]
    chunk_y = chunk_x // n_y
    chunk_z = chunk_y // dims["z"]
    count_all = batch * lax.axis_size("row") * lax.axis_size("col")
    rate = PROBE_RATE / math.sqrt(count_all)
    any_space = pl.BlockSpec(memory_space=pl.ANY)
    vmem = pl.BlockSpec(memory_space=pltpu.VMEM)
    smem = pl.BlockSpec(memory_space=pltpu.SMEM)

    def block(*shape, dtype=F32):
        return pltpu.VMEM(shape, dtype)

    tile = [block(3, 2, N, N) for _ in range(8)]
    arriving = [block(2, 2, N, N) for _ in range(4)]
    scratch = (
        tile
        + arriving
        + [
            block(batch, N, N, dtype=jnp.int32),
            block(8, N, 3 * N, dtype=BF16),
            block(8, 3 * N, N, dtype=BF16),
            block(batch, N, N),
            block(batch, 2, N, N),
            block(batch, 2, N, N),
            block(batch, 2, N, N),
            block(batch, 2, N, N),
            block(total, HALF),
            block(1, chunk_core, HALF),
            block(max(dims["x"] - 1, 1), chunk_x, HALF),
            block(max(n_y - 1, 1), chunk_y, HALF),
            block(max(dims["z"] - 1, 1), chunk_z, HALF),
            pltpu.SemaphoreType.DMA((7,)),
            pltpu.SemaphoreType.DMA((48,)),
            pltpu.SemaphoreType.DMA((48,)),
        ]
    )
    gradient, probe_sum = pl.pallas_call(
        functools.partial(kernel, batch, rate, dims),
        out_shape=(
            jax.ShapeDtypeStruct(transmission.shape, F32),
            jax.ShapeDtypeStruct((total, HALF), F32),
        ),
        in_specs=[smem, any_space, vmem, any_space, vmem, vmem, any_space, any_space]
        + [vmem] * 3,
        out_specs=(vmem, vmem),
        scratch_shapes=scratch,
        compiler_params=pltpu.CompilerParams(
            collective_id=0, has_side_effects=True, vmem_limit_bytes=62 * 2**20
        ),
        name="ptycho_step",
    )(
        place,
        transmission,
        probe,
        frames,
        lower_level,
        level_span,
        left,
        right,
        perm_rows,
        perm_cols,
        spread,
    )
    summed = probe_sum.reshape(2, 2, N, HALF).transpose(0, 2, 1, 3).reshape(2, N, N)
    return transmission - OBJECT_RATE * gradient, probe - rate * summed


def solution(mesh):
    in_specs = (
        P(None, None, "row", "col"),
        P(),
        P(("row", "col"), None),
        P(("row", "col"), None, None),
        P(("row", "col"), None, None),
        P(("row", "col"), None, None),
    )
    out_specs = (P(None, None, "row", "col"), P())
    return jax.shard_map(
        functools.partial(body, DIMS),
        mesh=mesh,
        in_specs=in_specs,
        out_specs=out_specs,
        check_vma=False,
    )
```

time: 760 us -> 169 us (0.22); the launches traced: 750 us -> 169 us
  waiting for transfers between devices: 231 us -> 0 us
  matrix products: 229 us -> 0 us
  local copies, waits for them, and re-layouts: 192 us -> 0.69 us
  Pallas kernels: 0 us -> 162 us
  loops' own time: 32.3 us -> 0 us
  other arithmetic: 37.8 us -> 5.84 us
  between operations: 14.8 us -> 0.67 us
  starting transfers between devices: 12.8 us -> 0 us
    dot_general x48 -> x0, matrix products: 229 us -> none  [the longest x12 59.3 us: transform(): real_mid = left(cosine, values[0]) - left(table_imag, values[1])]
    psum x1 -> x0, waiting for transfers between devices: 163 us -> none  [body(): probe_sum = lax.psum(probe_local, ('row', 'col'))]
    pallas_call x0 -> x1, Pallas kernels: none -> 162 us  [body(): pl.pallas_call(functools.partial(kernel, batch, rate, dims), out_shape=(j...]
    dynamic_update_slice x8 -> x0, local copies, waits for them, and re-layouts: 96.5 us -> none  [accumulate(): lax.dynamic_update_slice(total, current_patch + gradient_patches[position...]
    ppermute x4 -> x0, waiting for transfers between devices: 67.1 us -> none  [from_behind(): return lax.ppermute(x, axis, pairs)]
    gather x24 -> x0, local copies, waits for them, and re-layouts: 36.7 us -> none
    another operation x2 -> x0, loops' own time: 32.3 us -> none  [the longest x1 32.2 us: body(): lax.fori_loop(0, batch, accumulate, jnp.zeros(extended.shape, jnp.float32))]
    mul x2 -> x0, local copies, waits for them, and re-layouts: 19.4 us -> none  [intensity(): shaped * (extent[..., :, None, :, None] / 255.0)]
  transfers between devices with their start and end apart: 5 -> 0, of which waited for: 3 -> 0; matrix products, arithmetic and copies ran while one was open for 6% -> 0% of each run, Pallas kernels for 0% -> 0%
where the time goes in v1:
time: 169 us
  Pallas kernels  162 us (96%)
  other arithmetic  5.84 us (3%)
    pallas_call x1, Pallas kernels, body(): pl.pallas_call(functools.partial(kernel, batch, rate, dims), out_shape=(j...  162 us
    sub x2, other arithmetic, body(): return (transmission - OBJECT_RATE * gradient, probe - rate * summed)  4.98 us

profile of v1, /device:TPU:1, one launch (start us, length us, event | category | flops | bytes accessed | tf_op | source)
XLA Modules:
  0.0 169.0 jit_solution(348004452209318527)
XLA Ops:
  0.6 0.1 pad_add_fusion
  0.7 0.7 broadcast_subtract_fusion
  1.5 0.1 copy.15
  1.5 0.6 reshape.14.place_ref
  2.1 161.8 %ptycho_step.1 = (f32[2,2,256,512]{3,2,1,0:T(8,128)}, f32[1024,128]{1,0:T(8,128)}) custom-call(s32[16]{0:T(128)} %reshape.14.place_ref, f32[2,2,256,512]{3,2,1,0:T(8,128)} %trans_hbm.1, f32[2,256,256]{2,1,0:T(8,128)} %probe_ref.1, s32[8,256,256]{2,1,0:T(8,128)} %frames_hbm.1, s32[8,16,16]{2,1,0:T(8,128)} %lower_ref.1, s32[8,16,16]{2,1,0:T(8,128)} %span_ref.1, ...), custom_call_target="tpu_custom_call" | custom-call | tf_op jit(solution)/shard_map/ptycho_step/pallas_call | solution.py:587
  163.9 0.0 copy-start.1
  163.9 0.0 copy-start
  163.9 4.1 %multiply_subtract_fusion = f32[2,2,256,512]{3,2,1,0:T(8,128)} fusion(f32[2,2,256,512]{3,2,1,0:T(8,128)} %trans_hbm.1, f32[2,2,256,512]{3,2,1,0:T(8,128)} %get-tuple-element.4), kind=kLoop, calls=%fused_computation | loop fusion | flops 1048576 | bytes 6291456 | tf_op jit(solution)/shard_map/sub | solution.py:615
  168.0 0.0 copy-done.1
  168.1 0.0 copy-done
  168.1 0.9 bitcast_subtract_fusion
  (1 shorter events, 0.0 us)
Async XLA Ops:
  163.9 4.1 %copy-start.1 = (f32[1024,128]{1,0:T(8,128)S(1)}, f32[1024,128]{1,0:T(8,128)}, u32[]{:S(2)}) copy-start(f32[1024,128]{1,0:T(8,128)} %get-tuple-element.5) | copy-start | bytes 1572868
  163.9 4.2 %copy-start = (f32[2,256,256]{2,1,0:T(8,128)S(1)}, f32[2,256,256]{2,1,0:T(8,128)}, u32[]{:S(2)}) copy-start(f32[2,256,256]{2,1,0:T(8,128)} %probe_ref.1) | copy-start | bytes 1572868

commit v2 on v1

--- a/solution.py
+++ b/solution.py
@@ -17,6 +17,9 @@
 NBK = 16
 DIMS = dict(yh=2, z=4, yl=2, x=4, core=2)
 MESH = pl.DeviceIdType.MESH
+PIECES = ((0, 0, 256, False), (1, 0, 160, True))
+LONG = (1, 160, 96)
+N_SEMS = 64
 F32 = jnp.float32
 BF16 = jnp.bfloat16
 
@@ -164,6 +167,11 @@
     rin1,
     din0,
     din1,
+    relay_up,
+    relay_down,
+    long_up,
+    long_down,
+    side_mid,
     frames,
     left,
     right,
@@ -184,11 +192,13 @@
     own, bel = (own0, own1), (bel0, bel1)
     gown, gbel = (gown0, gown1), (gbel0, gbel1)
     rin, din = (rin0, rin1), (din0, din1)
+    relay, longs = (relay_up, relay_down), (long_up, long_down)
     n_z, n_x, n_yl, n_yh = dims["z"], dims["x"], dims["yl"], dims["yh"]
-    n_row, n_col = n_yh * n_z, n_yl * n_x * 2
+    n_core = dims["core"]
+    n_row, n_col = n_yh * n_z, n_yl * n_x * n_core
     row, col = lax.axis_index("row"), lax.axis_index("col")
     yh, z = row // n_z, row % n_z
-    yl, x, core = col // (2 * n_x), (col // 2) % n_x, col % 2
+    yl, x, core = col // (n_core * n_x), (col // n_core) % n_x, col % n_core
     y_digit = yh * n_yl + yl
     n_y = n_yh * n_yl
 
@@ -197,17 +207,24 @@
     up, down = (row - 1, col), (row + 1, col)
     lft, rgt = (row, col - 1), (row, col + 1)
 
+    turn = n_x * n_core
+
     def core_member(m):
-        return (row, yl * 2 * n_x + x * 2 + m)
+        return (row, (yl * n_x + x) * n_core + m)
 
     def x_member(m):
-        return (row, yl * 2 * n_x + m * 2 + core)
+        return (row, (yl * n_x + m) * n_core + core)
 
     def y_member(m):
-        return ((m // n_yl) * n_z + z, (m % n_yl) * 2 * n_x + x * 2 + core)
+        return ((m // n_yl) * n_z + z, ((m % n_yl) * n_x + x) * n_core + core)
 
     def z_member(m):
         return (yh * n_z + m, col)
+
+    numbers = {}
+
+    def number(*key):
+        return numbers.setdefault(key, len(numbers))
 
     def load(src, dst, i):
         return pltpu.make_async_copy(src, dst, local_sem.at[i])
@@ -241,7 +258,7 @@
             hail(dev)
 
     groups = (
-        (core_member, 2, core),
+        (core_member, n_core, core),
         (x_member, n_x, x),
         (y_member, n_y, y_digit),
         (z_member, n_z, z),
@@ -252,9 +269,32 @@
     hails = sum(size - 1 for _, size, _ in groups)
     for cond in (has_up, has_down, has_left, has_right):
         hails = hails + jnp.where(cond, 1, 0)
+    edges = ()
+    if n_yh > 1:
+        edges = (
+            (row, n_z + 2, (n_z - 1, col)),
+            (row, n_z - 1, (n_z + 2, col)),
+            (row, 1, (n_z, col)),
+            (row, n_z, (1, col)),
+        )
+    if n_yl > 1:
+        edges += (
+            (col, 0, (row, turn - 1)),
+            (col, turn - 1, (row, 0)),
+            (col, n_col - 1, (row, turn)),
+            (col, turn, (row, n_col - 1)),
+        )
+    for at, here, there in edges:
+
+        @pl.when(at == here)
+        def _(there=there):
+            hail(there)
+
+        hails = hails + jnp.where(at == here, 1, 0)
     pl.semaphore_wait(barrier, hails)
 
-    def remote(src, dst, i, dev):
+    def remote(src, dst, key, dev):
+        i = number(*key)
         return pltpu.make_async_remote_copy(
             src_ref=src,
             dst_ref=dst,
@@ -264,34 +304,182 @@
             device_id_type=MESH,
         )
 
-    def fwd_rows(s, c):
-        return remote(
-            trans_hbm.at[s, :, :, pl.ds(c * N, N)], bel[s].at[c], 8 * s + c, up
-        )
-
-    def fwd_side(s):
-        return remote(trans_hbm.at[s, :, :, pl.ds(0, N)], own[s].at[2], 8 * s + 2, lft)
-
-    def fwd_corner(s):
-        return remote(bel[s].at[0], bel[s].at[2], 8 * s + 3, lft)
-
-    def back_corner(s):
-        return remote(gbel[s].at[2], rin[s].at[1], 8 * s + 4, rgt)
-
-    def back_side(s):
-        return remote(gown[s].at[2], rin[s].at[0], 8 * s + 5, rgt)
-
-    def back_rows(s, c):
-        return remote(gbel[s].at[c], din[s].at[c], 8 * s + 6 + c, down)
-
     def on(cond, f):
         @pl.when(cond)
         def _():
             f()
 
-    for c in range(2):
-        on(has_up, fwd_rows(0, c).start)
-    on(has_left, fwd_side(0).start)
+    def both(*conds):
+        return functools.reduce(jnp.logical_and, conds)
+
+    n_pieces = len(PIECES)
+    split_rows = n_yh > 1
+
+    class Halo:
+        def __init__(self, way, s):
+            self.way, self.s = way, s
+            self.sends, self.takes = (has_up, has_down) if way < 0 else (has_down, has_up)
+            self.next = (row + way, col)
+            self.edge = n_z if way < 0 else n_z - 1
+            self.relay = n_row - 1 if way < 0 else 0
+            self.last = self.edge + way
+            self.ring = (yh * n_z + (z - way + n_z) % n_z, col)
+            self.from1 = yh * n_z + (z + way + n_z) % n_z
+            self.from2 = yh * n_z + (z + 2 * way + n_z) % n_z
+            none = 0 if way < 0 else n_row - 1
+            self.pass1 = jnp.logical_and(n_z > 2, self.from1 != none)
+            self.pass2 = jnp.logical_and(n_z > 2, self.from2 != none)
+
+        def ends(self, half, start, rows):
+            here = pl.ds(start, rows)
+            if self.way < 0:
+                src = trans_hbm.at[self.s, :, here, pl.ds(half * N, N)]
+                return src, bel[self.s].at[half, :, here]
+            return gbel[self.s].at[half, :, here], din[self.s].at[half, :, here]
+
+        def piece(self, k):
+            half, start, rows, _ = PIECES[k]
+            src, dst = self.ends(half, start, rows)
+            return remote(src, dst, ("piece", self.way, self.s, k), self.next)
+
+        def middle(self, k):
+            first = sum(p[2] for p in PIECES[:k] if p[3])
+            return relay[max(self.way, 0)].at[self.s, :, pl.ds(first, PIECES[k][2])]
+
+        def first_leg(self, k):
+            half, start, rows, _ = PIECES[k]
+            src, _ = self.ends(half, start, rows)
+            mid = self.middle(k)
+            return remote(src, mid, ("leg", self.way, self.s, k), (self.relay, col))
+
+        def second_leg(self, k):
+            half, start, rows, _ = PIECES[k]
+            _, dst = self.ends(half, start, rows)
+            mid = self.middle(k)
+            return remote(mid, dst, ("piece", self.way, self.s, k), (self.last, col))
+
+        def relayed(self, k):
+            return split_rows and PIECES[k][3]
+
+        def start_piece(self, k):
+            if not self.relayed(k):
+                on(self.sends, self.piece(k).start)
+                return
+            on(both(self.sends, row != self.edge), self.piece(k).start)
+            on(row == self.edge, self.first_leg(k).start)
+
+        def pass_on(self):
+            for k in range(n_pieces):
+                if self.relayed(k):
+
+                    @pl.when(row == self.relay)
+                    def _(k=k):
+                        self.first_leg(k).wait_recv()
+                        self.second_leg(k).start()
+
+        def wait_piece(self, k):
+            on(self.takes, self.piece(k).wait_recv)
+
+        def hop(self, h):
+            src, dst = self.ends(*LONG)
+            mids = longs[max(self.way, 0)]
+            src = src if h == 0 else mids.at[self.s, h - 1]
+            dst = dst if h == 2 else mids.at[self.s, h]
+            dev = (self.from2 + self.way, col) if h == 2 else self.ring
+            return remote(src, dst, ("long", self.way, self.s, h), dev)
+
+        def start_long(self):
+            on(self.sends, self.hop(0).start)
+
+        def pass_long(self, h):
+            @pl.when((self.pass1, self.pass2)[h])
+            def _():
+                self.hop(h).wait_recv()
+                self.hop(h + 1).start()
+
+        def wait_long(self):
+            on(self.takes, self.hop(2).wait_recv)
+
+        def finish(self):
+            for k in range(n_pieces):
+                if not self.relayed(k):
+                    on(self.sends, self.piece(k).wait_send)
+                    continue
+                on(both(self.sends, row != self.edge), self.piece(k).wait_send)
+                on(row == self.edge, self.first_leg(k).wait_send)
+                on(row == self.relay, self.second_leg(k).wait_send)
+            on(self.sends, self.hop(0).wait_send)
+            on(self.pass1, self.hop(1).wait_send)
+            on(self.pass2, self.hop(2).wait_send)
+
+    fwd = Halo(-1, 0), Halo(-1, 1)
+    back = Halo(1, 0), Halo(1, 1)
+
+    class Side:
+        def __init__(self, way, s):
+            self.way, self.s = way, s
+            self.sends, self.takes = (has_left, has_right) if way < 0 else (has_right, has_left)
+            self.edge = turn if way < 0 else turn - 1
+            self.relay = 0 if way < 0 else n_col - 1
+            self.mid = side_mid.at[max(way, 0), s]
+            if way < 0:
+                self.src, self.dst = trans_hbm.at[s, :, :, pl.ds(0, N)], own[s].at[2]
+            else:
+                self.src, self.dst = gown[s].at[2], rin[s].at[0]
+            self.relayed = n_yl > 1
+
+        def whole(self):
+            return remote(self.src, self.dst, ("side", self.way, self.s), (row, col + self.way))
+
+        def first_leg(self):
+            return remote(self.src, self.mid, ("side_leg", self.way, self.s), (row, self.relay))
+
+        def second_leg(self):
+            there = (row, self.edge + self.way)
+            return remote(self.mid, self.dst, ("side", self.way, self.s), there)
+
+        def start(self):
+            if not self.relayed:
+                on(self.sends, self.whole().start)
+                return
+            on(both(self.sends, col != self.edge), self.whole().start)
+            on(col == self.edge, self.first_leg().start)
+
+        def pass_on(self):
+            if self.relayed:
+
+                @pl.when(col == self.relay)
+                def _():
+                    self.first_leg().wait_recv()
+                    self.second_leg().start()
+
+        def wait(self):
+            on(self.takes, self.whole().wait_recv)
+
+        def finish(self):
+            if not self.relayed:
+                on(self.sends, self.whole().wait_send)
+                return
+            on(both(self.sends, col != self.edge), self.whole().wait_send)
+            on(col == self.edge, self.first_leg().wait_send)
+            on(col == self.relay, self.second_leg().wait_send)
+
+    fwd_side = Side(-1, 0), Side(-1, 1)
+    back_side = Side(1, 0), Side(1, 1)
+
+    def fwd_corner(s):
+        return remote(bel[s].at[0], bel[s].at[2], ("fwd_corner", s), lft)
+
+    def back_corner(s):
+        return remote(gbel[s].at[2], rin[s].at[1], ("back_corner", s), rgt)
+
+    late = [k for k in range(n_pieces) if PIECES[k][0] == 0]
+    early = [k for k in range(n_pieces) if PIECES[k][0] == 1]
+
+    fwd[0].start_long()
+    for k in late + early:
+        fwd[0].start_piece(k)
+    fwd_side[0].start()
 
     zero3 = jnp.zeros((2, N, N), F32)
     for s in range(2):
@@ -360,31 +548,25 @@
         return jnp.where(rows, here, below)
 
     def arrive(s):
-        @pl.when(has_down)
-        def _():
-            fwd_rows(s, 0).wait_recv()
-
-        @pl.when(jnp.logical_and(has_down, has_left))
-        def _():
-            fwd_corner(s).start()
-
-        if s == 0:
-            for c in range(2):
-                on(has_up, fwd_rows(1, c).start)
-            on(has_left, fwd_side(1).start)
-
-        @pl.when(has_down)
-        def _():
-            fwd_rows(s, 1).wait_recv()
-
-        @pl.when(has_right)
-        def _():
-            fwd_side(s).wait_recv()
-
-        @pl.when(jnp.logical_and(has_down, has_right))
-        def _():
-            fwd_corner(s).wait_recv()
-
+        for k in late:
+            fwd[s].wait_piece(k)
+        on(both(has_down, has_left), fwd_corner(s).start)
+        fwd[s].pass_on()
+        for k in early:
+            fwd[s].wait_piece(k)
+        fwd[s].wait_long()
+        fwd_side[s].wait()
+        on(both(has_down, has_right), fwd_corner(s).wait_recv)
+
+    fwd[0].pass_long(0)
+    fwd[1].start_long()
+    for k in late + early:
+        fwd[1].start_piece(k)
+    fwd_side[1].start()
+    fwd_side[0].pass_on()
+    fwd[0].pass_long(1)
+    fwd[1].pass_long(0)
+    fwd_side[1].pass_on()
     for c in loads[:4]:
         c.wait()
     arrive(0)
@@ -396,6 +578,7 @@
         wave = complex_mul((wav[j, 0], wav[j, 1]), patch)
         amp[j, 0], amp[j, 1] = transform(*wave, left, right, 0, True, True)
 
+    fwd[1].pass_long(1)
     arrive(1)
 
     @pl.loop(0, batch)
@@ -404,9 +587,9 @@
         incoming = amp[j, 0], amp[j, 1]
         far = transform(*complex_mul(incoming, patch), left, right, 1, True, False)
         misfit = far[0] * far[0] + far[1] * far[1] - meas[j]
-        back = transform(misfit * far[0], misfit * far[1], left, right, 2, False, True)
-        piece[j, 0], piece[j, 1] = conj_mul(back, incoming)
-        amp[j, 0], amp[j, 1] = conj_mul(back, patch)
+        wave = transform(misfit * far[0], misfit * far[1], left, right, 2, False, True)
+        piece[j, 0], piece[j, 1] = conj_mul(wave, incoming)
+        amp[j, 0], amp[j, 1] = conj_mul(wave, patch)
 
     def accumulate(s):
         @pl.loop(0, N // 8)
@@ -429,29 +612,33 @@
                     gbel[s][c, p, here, :] = sums[1][c]
 
     def send_back(s):
-        on(has_right, back_corner(s).start)
-        on(has_down, back_rows(s, 1).start)
-        on(has_right, back_side(s).start)
+        on(both(has_right, has_down), back_corner(s).start)
+        back[s].start_long()
+        for k in early:
+            back[s].start_piece(k)
+        back_side[s].start()
 
     def send_back_late(s):
-        @pl.when(has_left)
+        @pl.when(both(has_left, has_down))
         def _():
             back_corner(s).wait_recv()
-
-        gbel[s][0] += rin[s][1]
-        on(has_down, back_rows(s, 0).start)
+            gbel[s][0] += rin[s][1]
+
+        for k in late:
+            back[s].start_piece(k)
 
     accumulate(1)
     send_back(1)
-    send_back_late(1)
 
     gacc[...] = jnp.zeros_like(gacc)
 
     @pl.loop(0, batch)
     def _(j):
-        back = transform(amp[j, 0], amp[j, 1], left, right, 3, True, True)
-        piece[j, 0], piece[j, 1] = conj_mul(back, (wav[j, 0], wav[j, 1]))
-        term = conj_mul(back, (patch0[j, 0], patch0[j, 1]))
+        on(j == batch - 3, lambda: back[1].pass_long(0))
+        on(j == batch - 1, lambda: send_back_late(1))
+        wave = transform(amp[j, 0], amp[j, 1], left, right, 3, True, True)
+        piece[j, 0], piece[j, 1] = conj_mul(wave, (wav[j, 0], wav[j, 1]))
+        term = conj_mul(wave, (patch0[j, 0], patch0[j, 1]))
         y, x = place(j)
         for p in range(2):
             turned = pltpu.roll(pltpu.roll(term[p], (N - y) % N, 0), (N - x % N) % N, 1)
@@ -459,15 +646,15 @@
                 gacc[pl.ds((2 * p + h) * N, N), :] += turned[:, h * HALF : (h + 1) * HALF]
 
     accumulate(0)
+    back[1].pass_long(1)
     send_back(0)
-    send_back_late(0)
 
     total = gacc.shape[0]
     stages = (
-        (stage_core, core_member, 2, core, 16),
-        (stage_x, x_member, n_x, x, 18),
-        (stage_y, y_member, n_y, y_digit, 22),
-        (stage_z, z_member, n_z, z, 26),
+        (stage_core, core_member, n_core, core, "core"),
+        (stage_x, x_member, n_x, x, "x"),
+        (stage_y, y_member, n_y, y_digit, "y"),
+        (stage_z, z_member, n_z, z, "z"),
     )
     length = total
     base = 0
@@ -478,7 +665,7 @@
         for k in range(1, size):
             m = (me + k) % size
             src = gacc.at[pl.ds(pl.multiple_of(base + m * chunk, 8), chunk), :]
-            copies.append(remote(src, stage.at[k - 1], sem + k - 1, member(m)))
+            copies.append(remote(src, stage.at[k - 1], ("sum", sem, k), member(m)))
         for c in copies:
             c.start()
         spans.append((base, length, chunk))
@@ -491,6 +678,16 @@
             got = got + stage[k - 1]
         gacc[mine, :] = got
         length = chunk
+        if sem == "core":
+            back[1].pass_on()
+            back_side[1].pass_on()
+        if sem == "x":
+            send_back_late(0)
+        if sem == "y":
+            back[0].pass_long(0)
+        if sem == "z":
+            back[0].pass_on()
+            back_side[0].pass_on()
 
     mine = pl.ds(pl.multiple_of(base, 8), length)
     newprobe_ref[mine, :] = gacc[mine, :]
@@ -499,7 +696,7 @@
     ):
         held = newprobe_ref.at[pl.ds(pl.multiple_of(start + me * chunk, 8), chunk), :]
         copies = [
-            remote(held, held, 14 + sem + k - 1, member((me + k) % size))
+            remote(held, held, ("whole", sem, k), member((me + k) % size))
             for k in range(1, size)
         ]
         for c in copies:
@@ -508,20 +705,16 @@
             c.wait_send()
             m = (me - k + size) % size
             there = newprobe_ref.at[pl.ds(pl.multiple_of(start + m * chunk, 8), chunk), :]
-            remote(there, there, 14 + sem + k - 1, member(m)).wait_recv()
+            remote(there, there, ("whole", sem, k), member(m)).wait_recv()
+        if sem == "y":
+            back[0].pass_long(1)
 
     for s in (1, 0):
-
-        @pl.when(has_left)
-        def _(s=s):
-            back_side(s).wait_recv()
-
+        back_side[s].wait()
+        for k in range(n_pieces):
+            back[s].wait_piece(k)
+        back[s].wait_long()
         for c in range(2):
-
-            @pl.when(has_up)
-            def _(s=s, c=c):
-                back_rows(s, c).wait_recv()
-
             for p in range(2):
                 value = gown[s][c, p] + din[s][c, p]
                 if c == 0:
@@ -529,13 +722,13 @@
                 grad_ref[s, p, :, pl.ds(c * N, N)] = value
 
     for s in range(2):
-        for c in range(2):
-            on(has_up, fwd_rows(s, c).wait_send)
-            on(has_down, back_rows(s, c).wait_send)
-        on(has_left, fwd_side(s).wait_send)
-        on(jnp.logical_and(has_down, has_left), fwd_corner(s).wait_send)
-        on(has_right, back_corner(s).wait_send)
-        on(has_right, back_side(s).wait_send)
+        fwd[s].finish()
+        back[s].finish()
+        fwd_side[s].finish()
+        on(both(has_down, has_left), fwd_corner(s).wait_send)
+        on(both(has_right, has_down), back_corner(s).wait_send)
+        back_side[s].finish()
+    assert len(numbers) <= N_SEMS
 
 
 def body(dims, transmission, probe, offsets, frames, lower_level, level_span):
@@ -547,7 +740,7 @@
     perm_rows, perm_cols, spread = permutation()
     n_y = dims["yh"] * dims["yl"]
     total = 2 * 2 * N
-    chunk_core = total // 2
+    chunk_core = total // dims["core"]
     chunk_x = chunk_core // dims["x"]
     chunk_y = chunk_x // n_y
     chunk_z = chunk_y // dims["z"]
@@ -565,6 +758,9 @@
     scratch = (
         tile
         + arriving
+        + [block(2, 2, sum(p[2] for p in PIECES if p[3]), N) for _ in range(2)]
+        + [block(2, 2, 2, LONG[2], N) for _ in range(2)]
+        + [block(2, 2, 2, N, N)]
         + [
             block(batch, N, N, dtype=jnp.int32),
             block(8, N, 3 * N, dtype=BF16),
@@ -580,8 +776,8 @@
             block(max(n_y - 1, 1), chunk_y, HALF),
             block(max(dims["z"] - 1, 1), chunk_z, HALF),
             pltpu.SemaphoreType.DMA((7,)),
-            pltpu.SemaphoreType.DMA((48,)),
-            pltpu.SemaphoreType.DMA((48,)),
+            pltpu.SemaphoreType.DMA((N_SEMS,)),
+            pltpu.SemaphoreType.DMA((N_SEMS,)),
         ]
     )
     gradient, probe_sum = pl.pallas_call(

time: 169 us -> 133 us (0.79)
  Pallas kernels: 162 us -> 125 us
    pallas_call x1, Pallas kernels: 162 us -> 125 us  [body(): pl.pallas_call(functools.partial(kernel, batch, rate, dims), out_shape=(j...]
where the time goes in v2:
time: 133 us
  Pallas kernels  125 us (94%)
  other arithmetic  5.84 us (4%)
    pallas_call x1, Pallas kernels, body(): pl.pallas_call(functools.partial(kernel, batch, rate, dims), out_shape=(j...  125 us
    sub x2, other arithmetic, body(): return (transmission - OBJECT_RATE * gradient, probe - rate * summed)  4.98 us

profile of v2, /device:TPU:1, one launch (start us, length us, event | category | flops | bytes accessed | tf_op | source)
XLA Modules:
  0.0 132.7 jit_solution(9816777297539393277)
XLA Ops:
  0.6 0.1 pad_add_fusion
  0.7 0.7 broadcast_subtract_fusion
  1.5 0.1 copy.15
  1.5 0.6 reshape.14.place_ref
  2.1 125.4 %ptycho_step.1 = (f32[2,2,256,512]{3,2,1,0:T(8,128)}, f32[1024,128]{1,0:T(8,128)}) custom-call(s32[16]{0:T(128)} %reshape.14.place_ref, f32[2,2,256,512]{3,2,1,0:T(8,128)} %trans_hbm.1, f32[2,256,256]{2,1,0:T(8,128)} %probe_ref.1, s32[8,256,256]{2,1,0:T(8,128)} %frames_hbm.1, s32[8,16,16]{2,1,0:T(8,128)} %lower_ref.1, s32[8,16,16]{2,1,0:T(8,128)} %span_ref.1, ...), custom_call_target="tpu_custom_call" | custom-call | tf_op jit(solution)/shard_map/ptycho_step/pallas_call | solution.py:783
  127.6 0.0 copy-start.1
  127.6 0.0 copy-start
  127.6 4.1 %multiply_subtract_fusion = f32[2,2,256,512]{3,2,1,0:T(8,128)} fusion(f32[2,2,256,512]{3,2,1,0:T(8,128)} %trans_hbm.1, f32[2,2,256,512]{3,2,1,0:T(8,128)} %get-tuple-element.4), kind=kLoop, calls=%fused_computation | loop fusion | flops 1048576 | bytes 6291456 | tf_op jit(solution)/shard_map/sub | solution.py:811
  131.7 0.0 copy-done.1
  131.8 0.0 copy-done
  131.8 0.9 bitcast_subtract_fusion
  (1 shorter events, 0.0 us)
Async XLA Ops:
  127.6 4.1 %copy-start.1 = (f32[1024,128]{1,0:T(8,128)S(1)}, f32[1024,128]{1,0:T(8,128)}, u32[]{:S(2)}) copy-start(f32[1024,128]{1,0:T(8,128)} %get-tuple-element.5) | copy-start | bytes 1572868
  127.6 4.2 %copy-start = (f32[2,256,256]{2,1,0:T(8,128)S(1)}, f32[2,256,256]{2,1,0:T(8,128)}, u32[]{:S(2)}) copy-start(f32[2,256,256]{2,1,0:T(8,128)} %probe_ref.1) | copy-start | bytes 1572868

commit v3 on v2

--- a/solution.py
+++ b/solution.py
@@ -17,9 +17,10 @@
 NBK = 16
 DIMS = dict(yh=2, z=4, yl=2, x=4, core=2)
 MESH = pl.DeviceIdType.MESH
-PIECES = ((0, 0, 256, False), (1, 0, 160, True))
-LONG = (1, 160, 96)
-N_SEMS = 64
+PIECES = ((0, 0, 256, False), (1, 0, 168, True))
+LONG = (1, 168, 88)
+N_SEMS = 96
+GROUP = 2
 F32 = jnp.float32
 BF16 = jnp.bfloat16
 
@@ -130,6 +131,11 @@
     return along_rows(re, im, left_ref, op, pre, post)
 
 
+def transforms(waves, left_ref, right_ref, op, pre, post):
+    waves = [along_cols(*w, right_ref, op, pre, post) for w in waves]
+    return [along_rows(*w, left_ref, op, pre, post) for w in waves]
+
+
 def complex_mul(a, b):
     return a[0] * b[0] - a[1] * b[1], a[0] * b[1] + a[1] * b[0]
 
@@ -142,19 +148,19 @@
     batch,
     rate,
     dims,
-    place_ref,
+    offset_hbm,
     trans_hbm,
-    probe_ref,
+    probe_hbm,
     frames_hbm,
-    lower_ref,
-    span_ref,
+    lower_hbm,
+    span_hbm,
     left_hbm,
     right_hbm,
-    perm_rows_ref,
-    perm_cols_ref,
-    spread_ref,
-    grad_ref,
-    newprobe_ref,
+    perm_rows_hbm,
+    perm_cols_hbm,
+    spread_hbm,
+    newtrans_hbm,
+    newprobe_hbm,
     own0,
     own1,
     bel0,
@@ -172,18 +178,25 @@
     long_up,
     long_down,
     side_mid,
+    offset_ref,
     frames,
     left,
     right,
+    probe_ref,
+    lower_ref,
+    span_ref,
+    perm_rows_ref,
+    perm_cols_ref,
+    spread_ref,
     meas,
     wav,
     patch0,
     amp,
     piece,
     gacc,
+    gfull,
     stage_core,
-    stage_x,
-    stage_y,
+    stage_plane,
     stage_z,
     local_sem,
     send_sem,
@@ -212,11 +225,9 @@
     def core_member(m):
         return (row, (yl * n_x + x) * n_core + m)
 
-    def x_member(m):
-        return (row, (yl * n_x + m) * n_core + core)
-
-    def y_member(m):
-        return ((m // n_yl) * n_z + z, ((m % n_yl) * n_x + x) * n_core + core)
+    def plane_member(m):
+        y, x = m // n_x, m % n_x
+        return ((y // n_yl) * n_z + z, ((y % n_yl) * n_x + x) * n_core + core)
 
     def z_member(m):
         return (yh * n_z + m, col)
@@ -235,11 +246,19 @@
             loads.append(
                 load(trans_hbm.at[s, :, :, pl.ds(c * N, N)], own[s].at[c], 2 * s + c)
             )
-    loads.append(load(frames_hbm, frames, 4))
-    loads.append(load(left_hbm, left, 5))
-    loads.append(load(right_hbm, right, 6))
-    for c in loads:
-        c.start()
+    for src, dst in (
+        (offset_hbm, offset_ref),
+        (frames_hbm, frames),
+        (probe_hbm, probe_ref),
+        (lower_hbm, lower_ref),
+        (span_hbm, span_ref),
+        (perm_rows_hbm, perm_rows_ref),
+        (perm_cols_hbm, perm_cols_ref),
+        (spread_hbm, spread_ref),
+        (left_hbm, left),
+        (right_hbm, right),
+    ):
+        loads.append(load(src, dst, len(loads)))
 
     barrier = pltpu.get_barrier_semaphore()
 
@@ -259,8 +278,7 @@
 
     groups = (
         (core_member, n_core, core),
-        (x_member, n_x, x),
-        (y_member, n_y, y_digit),
+        (plane_member, n_y * n_x, y_digit * n_x + x),
         (z_member, n_z, z),
     )
     for member, size, me in groups:
@@ -364,9 +382,13 @@
         def start_piece(self, k):
             if not self.relayed(k):
                 on(self.sends, self.piece(k).start)
-                return
-            on(both(self.sends, row != self.edge), self.piece(k).start)
-            on(row == self.edge, self.first_leg(k).start)
+            else:
+                on(both(self.sends, row != self.edge), self.piece(k).start)
+
+        def start_legs(self):
+            for k in range(n_pieces):
+                if self.relayed(k):
+                    on(row == self.edge, self.first_leg(k).start)
 
         def pass_on(self):
             for k in range(n_pieces):
@@ -441,9 +463,12 @@
         def start(self):
             if not self.relayed:
                 on(self.sends, self.whole().start)
-                return
-            on(both(self.sends, col != self.edge), self.whole().start)
-            on(col == self.edge, self.first_leg().start)
+            else:
+                on(both(self.sends, col != self.edge), self.whole().start)
+
+        def start_leg(self):
+            if self.relayed:
+                on(col == self.edge, self.first_leg().start)
 
         def pass_on(self):
             if self.relayed:
@@ -477,9 +502,14 @@
     early = [k for k in range(n_pieces) if PIECES[k][0] == 1]
 
     fwd[0].start_long()
+    fwd[0].start_legs()
     for k in late + early:
         fwd[0].start_piece(k)
+    fwd_side[0].start_leg()
     fwd_side[0].start()
+
+    for c in loads:
+        c.start()
 
     zero3 = jnp.zeros((2, N, N), F32)
     for s in range(2):
@@ -504,12 +534,11 @@
             for c in range(2):
                 rin[s][c] = zero3
 
-    loads[4].wait()
-    for c in loads[5:]:
+    for c in loads[4:]:
         c.wait()
 
     def place(j):
-        return place_ref[2 * j], place_ref[2 * j + 1]
+        return offset_ref[0, j] & (N - 1), offset_ref[1, j] & (2 * N - 1)
 
     @pl.loop(0, batch)
     def _(j):
@@ -560,8 +589,10 @@
 
     fwd[0].pass_long(0)
     fwd[1].start_long()
+    fwd[1].start_legs()
     for k in late + early:
         fwd[1].start_piece(k)
+    fwd_side[1].start_leg()
     fwd_side[1].start()
     fwd_side[0].pass_on()
     fwd[0].pass_long(1)
@@ -581,42 +612,41 @@
     fwd[1].pass_long(1)
     arrive(1)
 
-    @pl.loop(0, batch)
-    def _(j):
-        patch = take(1, j, 0), take(1, j, 1)
-        incoming = amp[j, 0], amp[j, 1]
-        far = transform(*complex_mul(incoming, patch), left, right, 1, True, False)
-        misfit = far[0] * far[0] + far[1] * far[1] - meas[j]
-        wave = transform(misfit * far[0], misfit * far[1], left, right, 2, False, True)
-        piece[j, 0], piece[j, 1] = conj_mul(wave, incoming)
-        amp[j, 0], amp[j, 1] = conj_mul(wave, patch)
-
-    def accumulate(s):
+    @pl.loop(0, batch // GROUP)
+    def _(i):
+        js = [GROUP * i + k for k in range(GROUP)]
+        patches = [(take(1, j, 0), take(1, j, 1)) for j in js]
+        incoming = [(amp[j, 0], amp[j, 1]) for j in js]
+        far = [complex_mul(a, t) for a, t in zip(incoming, patches)]
+        far = transforms(far, left, right, 1, True, False)
+        misfit = [re * re + im * im - meas[j] for (re, im), j in zip(far, js)]
+        waves = [(m * re, m * im) for m, (re, im) in zip(misfit, far)]
+        waves = transforms(waves, left, right, 2, False, True)
+        for j, wave, a, t in zip(js, waves, incoming, patches):
+            piece[j, 0], piece[j, 1] = conj_mul(wave, a)
+            amp[j, 0], amp[j, 1] = conj_mul(wave, t)
+
+    def accumulate(s, below):
+        total = gbel[s] if below else gown[s]
+
         @pl.loop(0, N // 8)
         def _(i):
             here = pl.ds(pl.multiple_of(i * 8, 8), 8)
             rows = lax.broadcasted_iota(jnp.int32, (8, N), 0) + i * 8
             cols = lax.broadcasted_iota(jnp.int32, (8, N), 1)
+            sums = [[jnp.zeros((8, N), F32) for _ in range(3)] for _ in range(2)]
+            for j in range(batch):
+                y, x = place(j)
+                inside = rows < y if below else rows >= y
+                target = x // N + jnp.where(cols >= x % N, 0, 1)
+                target = jnp.where(inside, target, 3)
+                for c in range(3):
+                    there = target == c
+                    for p in range(2):
+                        sums[p][c] += jnp.where(there, piece[j, p, here, :], 0.0)
             for p in range(2):
-                sums = [[jnp.zeros((8, N), F32) for _ in range(3)] for _ in range(2)]
-                for j in range(batch):
-                    y, x = place(j)
-                    value = piece[j, p, here, :]
-                    target = x // N + jnp.where(cols >= x % N, 0, 1)
-                    upper = jnp.where(rows >= y, value, 0.0)
-                    for r, part in enumerate((upper, value - upper)):
-                        for c in range(3):
-                            sums[r][c] += jnp.where(target == c, part, 0.0)
                 for c in range(3):
-                    gown[s][c, p, here, :] = sums[0][c]
-                    gbel[s][c, p, here, :] = sums[1][c]
-
-    def send_back(s):
-        on(both(has_right, has_down), back_corner(s).start)
-        back[s].start_long()
-        for k in early:
-            back[s].start_piece(k)
-        back_side[s].start()
+                    total[c, p, here, :] = sums[p][c]
 
     def send_back_late(s):
         @pl.when(both(has_left, has_down))
@@ -627,99 +657,163 @@
         for k in late:
             back[s].start_piece(k)
 
-    accumulate(1)
-    send_back(1)
+    accumulate(1, True)
+    on(both(has_right, has_down), back_corner(1).start)
+    back[1].start_long()
+    back[1].start_legs()
+    for k in early:
+        back[1].start_piece(k)
+    accumulate(1, False)
+    back_side[1].start_leg()
+    back_side[1].start()
 
     gacc[...] = jnp.zeros_like(gacc)
 
-    @pl.loop(0, batch)
-    def _(j):
-        on(j == batch - 3, lambda: back[1].pass_long(0))
-        on(j == batch - 1, lambda: send_back_late(1))
-        wave = transform(amp[j, 0], amp[j, 1], left, right, 3, True, True)
-        piece[j, 0], piece[j, 1] = conj_mul(wave, (wav[j, 0], wav[j, 1]))
-        term = conj_mul(wave, (patch0[j, 0], patch0[j, 1]))
-        y, x = place(j)
+    @pl.loop(0, batch // GROUP)
+    def _(i):
+        on(i == batch // GROUP - 1, lambda: back[1].pass_long(0))
+        js = [GROUP * i + k for k in range(GROUP)]
+        waves = [(amp[j, 0], amp[j, 1]) for j in js]
+        first = [(wav[j, 0], wav[j, 1]) for j in js]
+        patches = [(patch0[j, 0], patch0[j, 1]) for j in js]
+        waves = transforms(waves, left, right, 3, True, True)
+        terms = [conj_mul(w, t) for w, t in zip(waves, patches)]
+        grads = [conj_mul(w, a) for w, a in zip(waves, first)]
         for p in range(2):
-            turned = pltpu.roll(pltpu.roll(term[p], (N - y) % N, 0), (N - x % N) % N, 1)
+            turned = 0.0
+            for j, term in zip(js, terms):
+                y, x = place(j)
+                turned += pltpu.roll(pltpu.roll(term[p], (N - y) % N, 0), (N - x % N) % N, 1)
             for h in range(2):
                 gacc[pl.ds((2 * p + h) * N, N), :] += turned[:, h * HALF : (h + 1) * HALF]
-
-    accumulate(0)
-    back[1].pass_long(1)
-    send_back(0)
-
-    total = gacc.shape[0]
-    stages = (
-        (stage_core, core_member, n_core, core, "core"),
-        (stage_x, x_member, n_x, x, "x"),
-        (stage_y, y_member, n_y, y_digit, "y"),
-        (stage_z, z_member, n_z, z, "z"),
-    )
-    length = total
-    base = 0
-    spans = []
-    for stage, member, size, me, sem in stages:
-        chunk = length // size
+        for j, grad in zip(js, grads):
+            piece[j, 0], piece[j, 1] = grad
+
+    send_back_late(1)
+
+    chunks = [gacc.shape[0]]
+    for _, size, _ in groups[:2]:
+        chunks.append(chunks[-1] // size)
+    starts = [0]
+    for chunk, (_, _, me) in zip(chunks[1:], groups):
+        starts.append(starts[-1] + me * chunk)
+    stages = stage_core, stage_plane
+
+    def part(ref, start, chunk):
+        return ref.at[pl.ds(pl.multiple_of(start, 8), chunk), :]
+
+    def scatter_start(g):
+        member, size, me = groups[g]
         copies = []
         for k in range(1, size):
             m = (me + k) % size
-            src = gacc.at[pl.ds(pl.multiple_of(base + m * chunk, 8), chunk), :]
-            copies.append(remote(src, stage.at[k - 1], ("sum", sem, k), member(m)))
+            src = part(gacc, starts[g] + m * chunks[g + 1], chunks[g + 1])
+            copies.append(remote(src, stages[g].at[k - 1], ("sum", g, k), member(m)))
         for c in copies:
             c.start()
-        spans.append((base, length, chunk))
-        base = base + me * chunk
-        mine = pl.ds(pl.multiple_of(base, 8), chunk)
+        return copies
+
+    def scatter_finish(g, copies):
         for c in copies:
             c.wait()
-        got = gacc[mine, :]
-        for k in range(1, size):
-            got = got + stage[k - 1]
-        gacc[mine, :] = got
-        length = chunk
-        if sem == "core":
-            back[1].pass_on()
-            back_side[1].pass_on()
-        if sem == "x":
-            send_back_late(0)
-        if sem == "y":
-            back[0].pass_long(0)
-        if sem == "z":
-            back[0].pass_on()
-            back_side[0].pass_on()
-
-    mine = pl.ds(pl.multiple_of(base, 8), length)
-    newprobe_ref[mine, :] = gacc[mine, :]
-    for (stage, member, size, me, sem), (start, length, chunk) in reversed(
-        list(zip(stages, spans))
-    ):
-        held = newprobe_ref.at[pl.ds(pl.multiple_of(start + me * chunk, 8), chunk), :]
+        mine = part(gacc, starts[g + 1], chunks[g + 1])
+        got = mine[...]
+        for k in range(1, groups[g][1]):
+            got = got + stages[g][k - 1]
+        mine[...] = got
+
+    def gather_start(g):
+        member, size, me = groups[g]
+        held = part(gfull, starts[g + 1], chunks[g + 1])
         copies = [
-            remote(held, held, ("whole", sem, k), member((me + k) % size))
+            remote(held, held, ("whole", g, k), member((me + k) % size))
             for k in range(1, size)
         ]
         for c in copies:
             c.start()
+        return copies
+
+    def gather_finish(g, copies):
+        member, size, me = groups[g]
         for k, c in enumerate(copies, 1):
             c.wait_send()
             m = (me - k + size) % size
-            there = newprobe_ref.at[pl.ds(pl.multiple_of(start + m * chunk, 8), chunk), :]
-            remote(there, there, ("whole", sem, k), member(m)).wait_recv()
-        if sem == "y":
-            back[0].pass_long(1)
-
-    for s in (1, 0):
-        back_side[s].wait()
-        for k in range(n_pieces):
-            back[s].wait_piece(k)
-        back[s].wait_long()
-        for c in range(2):
+            there = part(gfull, starts[g] + m * chunks[g + 1], chunks[g + 1])
+            remote(there, there, ("whole", g, k), member(m)).wait_recv()
+
+    stores = []
+
+    def finish_tile(s):
+        for c in (1, 0):
+            for k in late if c == 0 else early:
+                back[s].wait_piece(k)
+            if c == 0:
+                back_side[s].wait()
+            else:
+                back[s].wait_long()
             for p in range(2):
                 value = gown[s][c, p] + din[s][c, p]
                 if c == 0:
                     value = value + rin[s][0, p]
-                grad_ref[s, p, :, pl.ds(c * N, N)] = value
+                own[s][c, p] = own[s][c, p] - OBJECT_RATE * value
+            dst = newtrans_hbm.at[s, :, :, pl.ds(c * N, N)]
+            stores.append(load(own[s].at[c], dst, len(stores)))
+            stores[-1].start()
+
+    copies = scatter_start(0)
+    accumulate(0, True)
+    for k in early:
+        back[0].start_piece(k)
+    back[0].start_legs()
+    scatter_finish(0, copies)
+    copies = scatter_start(1)
+    on(both(has_right, has_down), back_corner(0).start)
+    back[1].pass_long(1)
+    back[0].start_long()
+    back[1].pass_on()
+    accumulate(0, False)
+    back_side[0].start_leg()
+    back_side[0].start()
+    scatter_finish(1, copies)
+
+    mine = part(gacc, starts[2], chunks[2])
+    copies = [
+        remote(mine, stage_z.at[z], ("sum", 3, k), z_member((z + k) % n_z))
+        for k in range(1, n_z)
+    ]
+    for c in copies:
+        c.start()
+    stage_z[z] = mine[...]
+    back_side[1].pass_on()
+    send_back_late(0)
+    back[0].pass_long(0)
+    back[0].pass_on()
+    for c in copies:
+        c.wait()
+    got = stage_z[0]
+    for m in range(1, n_z):
+        got = got + stage_z[m]
+    part(gfull, starts[2], chunks[2])[...] = got
+
+    copies = gather_start(1)
+    back_side[0].pass_on()
+    back[0].pass_long(1)
+    gather_finish(1, copies)
+    copies = gather_start(0)
+    finish_tile(1)
+    gather_finish(0, copies)
+
+    for p in range(2):
+        for h in range(2):
+            cols = pl.ds(h * HALF, HALF)
+            summed = gfull[pl.ds((2 * p + h) * N, N), :]
+            probe_ref[p, :, cols] = probe_ref[p, :, cols] - rate * summed
+    stores.append(load(probe_ref, newprobe_hbm, len(stores)))
+    stores[-1].start()
+
+    finish_tile(0)
+    for c in stores:
+        c.wait()
 
     for s in range(2):
         fwd[s].finish()
@@ -731,24 +825,38 @@
     assert len(numbers) <= N_SEMS
 
 
+def hand_on(trans, probe, out_trans, out_probe, held, held_probe, sems):
+    pieces = [(probe.at[p], held_probe.at[p], out_probe.at[p]) for p in range(2)]
+    for s in range(2):
+        for p in range(2):
+            for k in range(2):
+                at = s, p, pl.ds(k * HALF, HALF)
+                pieces.append((trans.at[at], held.at[at], out_trans.at[at]))
+    takes, gives = [], []
+    for i, (src, mid, dst) in enumerate(pieces):
+        takes.append(pltpu.make_async_copy(src, mid, sems.at[0, i]))
+        gives.append(pltpu.make_async_copy(mid, dst, sems.at[1, i]))
+    for take in takes:
+        take.start()
+    for take, give in zip(takes, gives):
+        take.wait()
+        give.start()
+    for give in gives:
+        give.wait()
+
+
 def body(dims, transmission, probe, offsets, frames, lower_level, level_span):
     batch = offsets.shape[0]
-    layers, _, rows, cols = transmission.shape
-    anchor = jnp.stack([lax.axis_index("row") * rows, lax.axis_index("col") * cols])
-    place = (offsets - anchor[None, :]).reshape(2 * batch)
     left, right = tables()
     perm_rows, perm_cols, spread = permutation()
     n_y = dims["yh"] * dims["yl"]
     total = 2 * 2 * N
     chunk_core = total // dims["core"]
-    chunk_x = chunk_core // dims["x"]
-    chunk_y = chunk_x // n_y
-    chunk_z = chunk_y // dims["z"]
+    members = n_y * dims["x"]
+    chunk_plane = chunk_core // members
     count_all = batch * lax.axis_size("row") * lax.axis_size("col")
     rate = PROBE_RATE / math.sqrt(count_all)
     any_space = pl.BlockSpec(memory_space=pl.ANY)
-    vmem = pl.BlockSpec(memory_space=pltpu.VMEM)
-    smem = pl.BlockSpec(memory_space=pltpu.SMEM)
 
     def block(*shape, dtype=F32):
         return pltpu.VMEM(shape, dtype)
@@ -762,40 +870,46 @@
         + [block(2, 2, 2, LONG[2], N) for _ in range(2)]
         + [block(2, 2, 2, N, N)]
         + [
+            pltpu.SMEM((2, batch), jnp.int32),
             block(batch, N, N, dtype=jnp.int32),
             block(8, N, 3 * N, dtype=BF16),
             block(8, 3 * N, N, dtype=BF16),
+            block(2, N, N),
+            block(batch, NBK, NBK, dtype=jnp.int32),
+            block(batch, NBK, NBK, dtype=jnp.int32),
+            block(N, N, dtype=BF16),
+            block(N, N, dtype=BF16),
+            block(NBK, N),
             block(batch, N, N),
             block(batch, 2, N, N),
             block(batch, 2, N, N),
             block(batch, 2, N, N),
             block(batch, 2, N, N),
             block(total, HALF),
+            block(total, HALF),
             block(1, chunk_core, HALF),
-            block(max(dims["x"] - 1, 1), chunk_x, HALF),
-            block(max(n_y - 1, 1), chunk_y, HALF),
-            block(max(dims["z"] - 1, 1), chunk_z, HALF),
-            pltpu.SemaphoreType.DMA((7,)),
+            block(max(members - 1, 1), chunk_plane, HALF),
+            block(dims["z"], chunk_plane, HALF),
+            pltpu.SemaphoreType.DMA((14,)),
             pltpu.SemaphoreType.DMA((N_SEMS,)),
             pltpu.SemaphoreType.DMA((N_SEMS,)),
         ]
     )
-    gradient, probe_sum = pl.pallas_call(
+    results = pl.pallas_call(
         functools.partial(kernel, batch, rate, dims),
         out_shape=(
             jax.ShapeDtypeStruct(transmission.shape, F32),
-            jax.ShapeDtypeStruct((total, HALF), F32),
+            jax.ShapeDtypeStruct(probe.shape, F32),
         ),
-        in_specs=[smem, any_space, vmem, any_space, vmem, vmem, any_space, any_space]
-        + [vmem] * 3,
-        out_specs=(vmem, vmem),
+        in_specs=[any_space] * 11,
+        out_specs=(any_space, any_space),
         scratch_shapes=scratch,
         compiler_params=pltpu.CompilerParams(
             collective_id=0, has_side_effects=True, vmem_limit_bytes=62 * 2**20
         ),
         name="ptycho_step",
     )(
-        place,
+        offsets.T,
         transmission,
         probe,
         frames,
@@ -807,8 +921,18 @@
         perm_cols,
         spread,
     )
-    summed = probe_sum.reshape(2, 2, N, HALF).transpose(0, 2, 1, 3).reshape(2, N, N)
-    return transmission - OBJECT_RATE * gradient, probe - rate * summed
+    return pl.pallas_call(
+        hand_on,
+        out_shape=tuple(jax.ShapeDtypeStruct(r.shape, r.dtype) for r in results),
+        in_specs=[any_space] * 2,
+        out_specs=(any_space, any_space),
+        scratch_shapes=[
+            block(*transmission.shape),
+            block(*probe.shape),
+            pltpu.SemaphoreType.DMA((2, 10)),
+        ],
+        name="hand_on",
+    )(*results)
 
 
 def solution(mesh):

time: 133 us -> 110 us (0.83)
  Pallas kernels: 125 us -> 108 us
  other arithmetic: 5.84 us -> 0 us
    pallas_call x1, Pallas kernels: 125 us -> 106 us  [body(): pl.pallas_call(functools.partial(kernel, batch, rate, dims), out_shape=(j...]
    sub x3 -> x0, other arithmetic: 5.73 us -> none  [the longest x2 4.98 us: body(): return (transmission - OBJECT_RATE * gradient, probe - rate * summed)]
    pallas_call x0 -> x1, Pallas kernels: none -> 2.6 us  [body(): pl.pallas_call(hand_on, out_shape=tuple((jax.ShapeDtypeStruct(r.shape, r....]
where the time goes in v3:
time: 110 us; the launch traced here: 109 us
  Pallas kernels  108 us (98%)
    pallas_call x1, Pallas kernels, body(): pl.pallas_call(functools.partial(kernel, batch, rate, dims), out_shape=(j...  106 us
    pallas_call x1, Pallas kernels, body(): pl.pallas_call(hand_on, out_shape=tuple((jax.ShapeDtypeStruct(r.shape, r....  2.6 us

profile of v3, /device:TPU:1, one launch (start us, length us, event | category | flops | bytes accessed | tf_op | source)
XLA Modules:
  0.0 108.9 jit_solution(18218576303103676074)
XLA Ops:
  0.6 105.7 %ptycho_step.1 = (f32[2,2,256,512]{3,2,1,0:T(8,128)}, f32[2,256,256]{2,1,0:T(8,128)}) custom-call(s32[2,8]{1,0:T(2,128)} %bitcast.1, f32[2,2,256,512]{3,2,1,0:T(8,128)} %trans_hbm.1, f32[2,256,256]{2,1,0:T(8,128)} %probe_hbm.1, s32[8,256,256]{2,1,0:T(8,128)} %frames_hbm.1, s32[8,16,16]{2,1,0:T(8,128)} %lower_hbm.1, s32[8,16,16]{2,1,0:T(8,128)} %span_hbm.1, ...), custom_call_target="tpu_custom_call" | custom-call | tf_op jit(solution)/shard_map/ptycho_step/pallas_call | solution.py:898
  106.3 2.6 %hand_on.1 = (f32[2,2,256,512]{3,2,1,0:T(8,128)}, f32[2,256,256]{2,1,0:T(8,128)}) custom-call(f32[2,2,256,512]{3,2,1,0:T(8,128)} %get-tuple-element.4.trans, f32[2,256,256]{2,1,0:T(8,128)} %get-tuple-element.5.probe), custom_call_target="tpu_custom_call" | custom-call | tf_op jit(solution)/shard_map/hand_on/pallas_call | solution.py:924

commit v4 on v3

--- a/solution.py
+++ b/solution.py
@@ -17,7 +17,7 @@
 NBK = 16
 DIMS = dict(yh=2, z=4, yl=2, x=4, core=2)
 MESH = pl.DeviceIdType.MESH
-PIECES = ((0, 0, 256, False), (1, 0, 168, True))
+PIECES = ((0, 0, 48, False), (0, 48, 208, False), (1, 0, 168, True))
 LONG = (1, 168, 88)
 N_SEMS = 96
 GROUP = 2
@@ -654,7 +654,10 @@
             back_corner(s).wait_recv()
             gbel[s][0] += rin[s][1]
 
-        for k in late:
+        back[s].start_piece(late[0])
+
+    def send_back_last(s):
+        for k in late[1:]:
             back[s].start_piece(k)
 
     accumulate(1, True)
@@ -690,6 +693,7 @@
             piece[j, 0], piece[j, 1] = grad
 
     send_back_late(1)
+    send_back_last(1)
 
     chunks = [gacc.shape[0]]
     for _, size, _ in groups[:2]:
@@ -774,6 +778,10 @@
     accumulate(0, False)
     back_side[0].start_leg()
     back_side[0].start()
+    back_side[1].pass_on()
+    send_back_late(0)
+    back[0].pass_long(0)
+    back[0].pass_on()
     scatter_finish(1, copies)
 
     mine = part(gacc, starts[2], chunks[2])
@@ -784,10 +792,7 @@
     for c in copies:
         c.start()
     stage_z[z] = mine[...]
-    back_side[1].pass_on()
-    send_back_late(0)
-    back[0].pass_long(0)
-    back[0].pass_on()
+    send_back_last(0)
     for c in copies:
         c.wait()
     got = stage_z[0]
@@ -796,8 +801,8 @@
     part(gfull, starts[2], chunks[2])[...] = got
 
     copies = gather_start(1)
+    back[0].pass_long(1)
     back_side[0].pass_on()
-    back[0].pass_long(1)
     gather_finish(1, copies)
     copies = gather_start(0)
     finish_tile(1)

time: 110 us -> 109 us (level); the launches traced: 109 us -> 109 us
  no operation moved by 1% of the time
where the time goes in v4:
time: 109 us
  Pallas kernels  108 us (99%)
    pallas_call x1, Pallas kernels, body(): pl.pallas_call(functools.partial(kernel, batch, rate, dims), out_shape=(j...  106 us
    pallas_call x1, Pallas kernels, body(): pl.pallas_call(hand_on, out_shape=tuple((jax.ShapeDtypeStruct(r.shape, r....  2.6 us

profile of v4, /device:TPU:1, one launch (start us, length us, event | category | flops | bytes accessed | tf_op | source)
XLA Modules:
  0.0 109.1 jit_solution(7243972212846155761)
XLA Ops:
  0.6 105.9 %ptycho_step.1 = (f32[2,2,256,512]{3,2,1,0:T(8,128)}, f32[2,256,256]{2,1,0:T(8,128)}) custom-call(s32[2,8]{1,0:T(2,128)} %bitcast.1, f32[2,2,256,512]{3,2,1,0:T(8,128)} %trans_hbm.1, f32[2,256,256]{2,1,0:T(8,128)} %probe_hbm.1, s32[8,256,256]{2,1,0:T(8,128)} %frames_hbm.1, s32[8,16,16]{2,1,0:T(8,128)} %lower_hbm.1, s32[8,16,16]{2,1,0:T(8,128)} %span_hbm.1, ...), custom_call_target="tpu_custom_call" | custom-call | tf_op jit(solution)/shard_map/ptycho_step/pallas_call | solution.py:903
  106.5 2.6 %hand_on.1 = (f32[2,2,256,512]{3,2,1,0:T(8,128)}, f32[2,256,256]{2,1,0:T(8,128)}) custom-call(f32[2,2,256,512]{3,2,1,0:T(8,128)} %get-tuple-element.4.trans, f32[2,256,256]{2,1,0:T(8,128)} %get-tuple-element.5.probe), custom_call_target="tpu_custom_call" | custom-call | tf_op jit(solution)/shard_map/hand_on/pallas_call | solution.py:929
